TPU v7x, 32 devices: a whole 2x2x4 slice. The times are simulated.
32 devices in a mesh: gx: 4 (over x, core), gy: 8 (over z, y).
Axes of the slice: x: 2, y: 2, z: 4, core: 2. Of those that a mesh axis runs over, the one named last changes fastest.
Arguments:
- state: float32 [16, 256, 1024], P(None, 'gx', 'gy'), may hold values from -5.5 to 5.5
- kappa_x: float32 [16, 256, 1024], P(None, 'gx', 'gy'), may hold values from 300 to 30000
- kappa_y: float32 [16, 256, 1024], P(None, 'gx', 'gy'), may hold values from 300 to 30000
Outputs:
- updated: float32 [16, 256, 1024], P(None, 'gx', 'gy')
All inputs are finite; a program needn't handle non-finite values.
Results may differ from a plain program's by a relative error of at most 0.025.
Values sent between devices are 32-bit elements; how exact they have to be, the bound alone decides.
A program may use at most 128 MiB of HBM per device.

v0:
```python
import jax
import jax.numpy as jnp
from jax import lax
from jax.sharding import PartitionSpec as P


def padded(cells, sides, width):
    for axis, dim in sides:
        count = lax.axis_size(axis)
        ends = count - 1
        head = lax.slice_in_dim(cells, 0, width, axis=dim)
        tail = lax.slice_in_dim(cells, cells.shape[dim] - width, cells.shape[dim], axis=dim)
        cells = jnp.concatenate(
            [
                lax.ppermute(tail, axis, [(i, (i + 1) % count) for i in range(ends)]),
                cells,
                lax.ppermute(head, axis, [((i + 1) % count, i) for i in range(ends)]),
            ],
            axis=dim,
        )
    return cells


def neighbor(values, step, axis):
    length = values.shape[axis]
    widths = [(0, 0)] * values.ndim
    if step > 0:
        part = lax.slice_in_dim(values, step, length, axis=axis)
        widths[axis] = (0, step)
    else:
        part = lax.slice_in_dim(values, 0, length + step, axis=axis)
        widths[axis] = (-step, 0)
    return jnp.pad(part, widths)


def reduce_lines(lower, diag, upper, sources, axis):
    lower = lower / diag
    upper = upper / diag
    sources = [entry / diag for entry in sources]
    length = diag.shape[axis]
    stride = 1
    while stride < length:
        low_prev = neighbor(lower, -stride, axis)
        up_prev = neighbor(upper, -stride, axis)
        low_next = neighbor(lower, stride, axis)
        up_next = neighbor(upper, stride, axis)
        pivot = 1.0 - lower * up_prev - upper * low_next
        sources = [
            (entry - lower * neighbor(entry, -stride, axis) - upper * neighbor(entry, stride, axis))
            / pivot
            for entry in sources
        ]
        lower, upper = (-lower * low_prev / pivot, -upper * up_next / pivot)
        stride = stride * 2
    return sources


def gathered_solve(allrows, position):
    sequence = jnp.moveaxis(allrows, 1, 0)
    zeros = jnp.zeros(allrows.shape[2:], jnp.float32)

    def forward(carry, row):
        prior_c, prior_d = carry
        pivot = row[1] - row[0] * prior_c
        next_c = row[2] / pivot
        next_d = (row[3] - row[0] * prior_d) / pivot
        return ((next_c, next_d), (next_c, next_d))

    final, (ratios, values) = lax.scan(forward, (zeros, zeros), sequence)

    def backward(later, pair):
        result = pair[1] - pair[0] * later
        return (result, result)

    final, solved = lax.scan(backward, zeros, (ratios, values), reverse=True)
    return lax.dynamic_slice_in_dim(solved, 2 * position, 2, 0)


def interface_x(rows):
    return gathered_solve(lax.all_gather(rows, "gx", axis=1, tiled=True), lax.axis_index("gx"))


def interface_y(rows):
    return gathered_solve(lax.all_gather(rows, "gy", axis=1, tiled=True), lax.axis_index("gy"))


def solve_line(left, right, source, axis, interface):
    lower = -left
    upper = -right
    diag = 1.0 + left + right
    length = diag.shape[axis]
    inner_lower = lax.slice_in_dim(lower, 1, length - 1, axis=axis)
    inner_diag = lax.slice_in_dim(diag, 1, length - 1, axis=axis)
    inner_upper = lax.slice_in_dim(upper, 1, length - 1, axis=axis)
    inner_source = lax.slice_in_dim(source, 1, length - 1, axis=axis)
    row_index = lax.broadcasted_iota(jnp.int32, inner_diag.shape, axis)
    first_row = row_index == 0
    last_row = row_index == length - 3
    zero = jnp.zeros_like(inner_diag)
    from_first = jnp.where(first_row, -inner_lower, zero)
    from_last = jnp.where(last_row, -inner_upper, zero)
    inner_lower = jnp.where(first_row, zero, inner_lower)
    inner_upper = jnp.where(last_row, zero, inner_upper)
    base, with_first, with_last = reduce_lines(
        inner_lower, inner_diag, inner_upper, [inner_source, from_first, from_last], axis
    )
    plane_shape = tuple((extent for position, extent in enumerate(diag.shape) if position != axis))

    def pick(values, position):
        return lax.index_in_dim(values, position, axis, keepdims=False).reshape(-1)

    lower_first, diag_first, upper_first, source_first = (
        pick(lower, 0),
        pick(diag, 0),
        pick(upper, 0),
        pick(source, 0),
    )
    lower_last, diag_last, upper_last, source_last = (
        pick(lower, length - 1),
        pick(diag, length - 1),
        pick(upper, length - 1),
        pick(source, length - 1),
    )
    coef_a = jnp.stack([lower_first, lower_last * pick(with_first, length - 3)])
    coef_b = jnp.stack(
        [
            diag_first + upper_first * pick(with_first, 0),
            diag_last + lower_last * pick(with_last, length - 3),
        ]
    )
    coef_c = jnp.stack([upper_first * pick(with_last, 0), upper_last])
    coef_d = jnp.stack(
        [
            source_first - upper_first * pick(base, 0),
            source_last - lower_last * pick(base, length - 3),
        ]
    )
    edges = interface(jnp.stack([coef_a, coef_b, coef_c, coef_d]))
    edge_first = jnp.expand_dims(edges[0].reshape(plane_shape), axis)
    edge_last = jnp.expand_dims(edges[1].reshape(plane_shape), axis)
    interior = base + with_first * edge_first + with_last * edge_last
    return jnp.concatenate([edge_first, interior, edge_last], axis=axis)


def on_device(state, kappa_x, kappa_y):
    wide_x = padded(jnp.stack([state, kappa_x]), (("gx", 2),), 1)
    field_x = wide_x[0]
    kappa_wx = wide_x[1]
    left_x = 0.5 * (kappa_wx[:, :-2] + kappa_wx[:, 1:-1])
    right_x = 0.5 * (kappa_wx[:, 1:-1] + kappa_wx[:, 2:])
    lap_x = right_x * (field_x[:, 2:] - state) - left_x * (state - field_x[:, :-2])
    wide_y = padded(jnp.stack([state, kappa_y]), (("gy", 3),), 1)
    field_y = wide_y[0]
    kappa_wy = wide_y[1]
    left_y = 0.5 * (kappa_wy[:, :, :-2] + kappa_wy[:, :, 1:-1])
    right_y = 0.5 * (kappa_wy[:, :, 1:-1] + kappa_wy[:, :, 2:])
    lap_y = right_y * (field_y[:, :, 2:] - state) - left_y * (state - field_y[:, :, :-2])
    source = state + lap_x + 2.0 * lap_y
    middle = solve_line(left_x, right_x, source, 1, interface_x)
    return solve_line(left_y, right_y, middle - lap_y, 2, interface_y)


def solution(mesh):
    return jax.shard_map(
        on_device,
        mesh=mesh,
        in_specs=(P(None, "gx", "gy"), P(None, "gx", "gy"), P(None, "gx", "gy")),
        out_specs=P(None, "gx", "gy"),
        check_vma=False,
    )
```

profile of v0, /device:TPU:0, one launch (start us, length us, event | category | flops | bytes accessed | tf_op | source)
XLA Modules:
  0.0 134.4 jit_solution(17219622964329688342)
XLA Ops:
  0.0 1.9 %copy_bitcast_fusion = (f32[1,16,64,128]{3,1,2,0:T(8,128)S(1)}, f32[1,16,64,128]{3,1,2,0:T(8,128)S(1)}) fusion(f32[16,64,128]{2,1,0:T(8,128)} %param.12, f32[16,64,128]{2,1,0:T(8,128)} %param.11), kind=kLoop, calls=%fused_computation.72 | loop fusion | bytes 2097152 | tf_op jit(solution)/shard_map/stack | solution.py:146
  1.9 2.4 %collective-permute-start.2 = (f32[2,16,1,128]{3,1,2,0:T(8,128)S(1)}, f32[2,16,1,128]{3,1,2,0:T(8,128)S(1)}, u32[]{:S(2)}, u32[]{:S(2)}) collective-permute-start(f32[2,16,1,128]{3,1,2,0:T(8,128)S(1)} %get-tuple-element.513), channel_id=1, source_target_pairs={{0,8},{8,16},{16,24},{1,9},{9,17},{17,25},{2,10},{10,18},{18,26},{... | collective-permute-start | bytes 49160 | tf_op jit(solution)/shard_map/ppermute | solution.py:15
  4.2 1.3 collective-permute-start.3
  5.9 1.4 %fusion.10 = (f32[2,16,64,1]{3,1,2,0:T(8,128)}, f32[2,16,64,1]{3,1,2,0:T(8,128)S(1)}) fusion(f32[1,16,64,128]{3,1,2,0:T(8,128)S(1)} %get-tuple-element.675, f32[1,16,64,128]{3,1,2,0:T(8,128)S(1)} %bitcast.118), kind=kLoop, calls=%fused_computation.32 | loop fusion | flops 4096 | bytes 1064960 | tf_op jit(solution)/shard_map/stack | solution.py:152
  7.2 1.7 %copy.21 = f32[2,16,64,1]{2,1,3,0:T(8,128)S(1)} copy(f32[2,16,64,1]{3,1,2,0:T(8,128)} %get-tuple-element.515) | data formatting | bytes 16384 | tf_op jit(solution)/shard_map/slice | solution.py:12
  8.9 4.2 %collective-permute-start = (f32[2,16,64,1]{2,1,3,0:T(8,128)S(1)}, f32[2,16,64,1]{2,1,3,0:T(8,128)S(1)}, u32[]{:S(2)}, u32[]{:S(2)}) collective-permute-start(f32[2,16,64,1]{2,1,3,0:T(8,128)S(1)} %copy.21), channel_id=1, source_target_pairs={{0,1},{1,2},{2,3},{3,4},{4,5},{5,6},{6,7},{8,9},{9,10},{10,11},{11... | collective-permute-start | bytes 24584 | tf_op jit(solution)/shard_map/ppermute | solution.py:15
  13.6 1.3 collective-permute-start.1
  15.5 3.7 %collective-permute-done.1 = f32[2,16,64,1]{2,1,3,0:T(8,128)S(1)} collective-permute-done((f32[2,16,64,1]{2,1,3,0:T(8,128)S(1)}, f32[2,16,64,1]{2,1,3,0:T(8,128)S(1)}, u32[]{:S(2)}, u32[]{:S(2)}) %collective-permute-start.1) | collective-permute-done | bytes 8224 | tf_op jit(solution)/shard_map/ppermute | solution.py:17
  19.2 1.4 %copy.24 = f32[2,16,64,1]{3,1,2,0:T(8,128)} copy(f32[2,16,64,1]{2,1,3,0:T(8,128)S(1)} %collective-permute-done.1) | data formatting | bytes 16384 | tf_op jit(solution)/shard_map/ppermute | solution.py:17
  20.7 2.1 %pad_maximum_fusion = f32[2,16,64,130]{3,1,2,0:T(8,128)S(1)} fusion(f32[2,16,64,1]{3,1,2,0:T(8,128)} %copy.24, f32[1,16,64,128]{3,1,2,0:T(8,128)S(1)} %bitcast.119, f32[1,16,64,128]{3,1,2,0:T(8,128)S(1)} %get-tuple-element.675, f32[2,16,64,1]{3,1,2,0:T(8,128)S(1)} %copy.23), kind=kLoop, calls=%fused_computation.28 | loop fusion | flops 798720 | bytes 2129920 | tf_op jit(solution)/shard_map/concatenate | solution.py:13
  23.3 0.9 copy-done.4
  24.2 1.4 %fusion.19 = (f32[16,64,128]{2,0,1:T(8,128)S(1)}, f32[16,64,128]{2,0,1:T(8,128)}, f32[16,64,128]{2,0,1:T(8,128)S(1)}, f32[16,64,128]{2,0,1:T(8,128)S(1)}, f32[16,64,128]{2,0,1:T(8,128)S(1)}) fusion(f32[16,66,128]{2,0,1:T(8,128)S(1)} %get-tuple-element.487, f32[16,64,128]{2,1,0:T(8,128)S(1)} %copy-done.4, f32[16,66,128]{2,0,1:T(8,128)S(1)} %get-tuple-element.486, ...), kind=kLoop, calls=%fused_computation.53 | loop fusion | flops 3276800 | bytes 8388608 | tf_op jit(solution)/shard_map/add | solution.py:158
  32.3 8.3 %all_gather.6 = f32[4,8,2048]{2,0,1:T(4,128)S(1)} all-gather(f32[4,2,2048]{2,0,1:T(4,128)S(1)} %copy.37), channel_id=1, replica_groups=mesh['gx'=4,'gy'=8] {'gx'}, dimensions={1}, use_global_device_ids=true | all-gather | bytes 327680 | tf_op jit(solution)/shard_map/all_gather | solution.py:80
  41.3 14.0 %while.68 = (s32[]{:T(128)}, f32[2048]{0:T(1024)S(1)}, f32[2048]{0:T(1024)S(1)}, f32[8,2048]{1,0:T(8,128)S(1)}, f32[8,2048]{1,0:T(8,128)}, /*index=5*/f32[8,4,20...) while((s32[]{:T(128)}, f32[2048]{0:T(1024)S(1)}, f32[2048]{0:T(1024)S(1)}, ...), condition=%wide.region_1.2_spmd.clone, body=%wide.region_0.1_spmd.clone.sunk | while | flops 16390 | bytes 164019 | solution.py:69
  41.3 1.5 %dynamic_update_slice.45 = f32[8,2048]{1,0:T(8,128)} dynamic-update-slice(f32[8,2048]{1,0:T(8,128)} %get-tuple-element.863, f32[1,2048]{1,0:T(1,128)S(1)} %bitcast.129, s32[]{:T(128)} %get-tuple-element.859, s32[]{:T(128)} %constant.120.clone.1..sunk) | dynamic-update-slice | bytes 16388 | tf_op jit(solution)/shard_map/while/body/jit(dynamic_update_index_in_dim)/dynamic_update_slice | solution.py:69
  43.1 1.5 %dynamic_update_slice.45 = f32[8,2048]{1,0:T(8,128)} dynamic-update-slice(f32[8,2048]{1,0:T(8,128)} %get-tuple-element.863, f32[1,2048]{1,0:T(1,128)S(1)} %bitcast.129, s32[]{:T(128)} %get-tuple-element.859, s32[]{:T(128)} %constant.120.clone.1..sunk) | dynamic-update-slice | bytes 16388 | tf_op jit(solution)/shard_map/while/body/jit(dynamic_update_index_in_dim)/dynamic_update_slice | solution.py:69
  44.8 1.5 %dynamic_update_slice.45 = f32[8,2048]{1,0:T(8,128)} dynamic-update-slice(f32[8,2048]{1,0:T(8,128)} %get-tuple-element.863, f32[1,2048]{1,0:T(1,128)S(1)} %bitcast.129, s32[]{:T(128)} %get-tuple-element.859, s32[]{:T(128)} %constant.120.clone.1..sunk) | dynamic-update-slice | bytes 16388 | tf_op jit(solution)/shard_map/while/body/jit(dynamic_update_index_in_dim)/dynamic_update_slice | solution.py:69
  46.6 1.5 %dynamic_update_slice.45 = f32[8,2048]{1,0:T(8,128)} dynamic-update-slice(f32[8,2048]{1,0:T(8,128)} %get-tuple-element.863, f32[1,2048]{1,0:T(1,128)S(1)} %bitcast.129, s32[]{:T(128)} %get-tuple-element.859, s32[]{:T(128)} %constant.120.clone.1..sunk) | dynamic-update-slice | bytes 16388 | tf_op jit(solution)/shard_map/while/body/jit(dynamic_update_index_in_dim)/dynamic_update_slice | solution.py:69
  48.3 1.5 %dynamic_update_slice.45 = f32[8,2048]{1,0:T(8,128)} dynamic-update-slice(f32[8,2048]{1,0:T(8,128)} %get-tuple-element.863, f32[1,2048]{1,0:T(1,128)S(1)} %bitcast.129, s32[]{:T(128)} %get-tuple-element.859, s32[]{:T(128)} %constant.120.clone.1..sunk) | dynamic-update-slice | bytes 16388 | tf_op jit(solution)/shard_map/while/body/jit(dynamic_update_index_in_dim)/dynamic_update_slice | solution.py:69
  50.1 1.5 %dynamic_update_slice.45 = f32[8,2048]{1,0:T(8,128)} dynamic-update-slice(f32[8,2048]{1,0:T(8,128)} %get-tuple-element.863, f32[1,2048]{1,0:T(1,128)S(1)} %bitcast.129, s32[]{:T(128)} %get-tuple-element.859, s32[]{:T(128)} %constant.120.clone.1..sunk) | dynamic-update-slice | bytes 16388 | tf_op jit(solution)/shard_map/while/body/jit(dynamic_update_index_in_dim)/dynamic_update_slice | solution.py:69
  51.8 1.5 %dynamic_update_slice.45 = f32[8,2048]{1,0:T(8,128)} dynamic-update-slice(f32[8,2048]{1,0:T(8,128)} %get-tuple-element.863, f32[1,2048]{1,0:T(1,128)S(1)} %bitcast.129, s32[]{:T(128)} %get-tuple-element.859, s32[]{:T(128)} %constant.120.clone.1..sunk) | dynamic-update-slice | bytes 16388 | tf_op jit(solution)/shard_map/while/body/jit(dynamic_update_index_in_dim)/dynamic_update_slice | solution.py:69
  53.6 1.5 %dynamic_update_slice.45 = f32[8,2048]{1,0:T(8,128)} dynamic-update-slice(f32[8,2048]{1,0:T(8,128)} %get-tuple-element.863, f32[1,2048]{1,0:T(1,128)S(1)} %bitcast.129, s32[]{:T(128)} %get-tuple-element.859, s32[]{:T(128)} %constant.120.clone.1..sunk) | dynamic-update-slice | bytes 16388 | tf_op jit(solution)/shard_map/while/body/jit(dynamic_update_index_in_dim)/dynamic_update_slice | solution.py:69
  55.3 9.0 %while.69 = (s32[]{:T(128)}, f32[2048]{0:T(1024)S(1)}, f32[8,2048]{1,0:T(8,128)S(1)}, f32[8,2048]{1,0:T(8,128)}, f32[8,2048]{1,0:T(8,128)S(1)}, /*index=5*/s32[]{:T(128)}, s32[]{:T(128)}, s32[]{:T(128)}) while((s32[]{:T(128)}, f32[2048]{0:T(1024)S(1)}, f32[8,2048]{1,0:T(8,128)S(1)}, f32[8,2048]{1,0:T(8,128)}, ...), condition=%wide.region_3.4_spmd.clone, body=%wide.region_2.3_spmd.clone.sunk | while | flops 6148 | bytes 82035 | solution.py:75
  55.3 0.9 constant_dynamic-slice_fusion.23
  56.4 0.9 constant_dynamic-slice_fusion.23
  57.5 0.9 constant_dynamic-slice_fusion.23
  58.6 0.9 constant_dynamic-slice_fusion.23
  59.7 0.9 constant_dynamic-slice_fusion.23
  60.8 0.9 constant_dynamic-slice_fusion.23
  62.0 0.9 constant_dynamic-slice_fusion.23
  63.1 0.9 constant_dynamic-slice_fusion.23
  64.5 0.9 copy-done
  69.5 0.7 subtract_divide_fusion.12
  73.7 0.7 subtract_divide_fusion.10
  75.7 0.7 subtract_divide_fusion.9
  77.8 0.7 subtract_divide_fusion.8
  79.3 0.9 subtract_divide_fusion.14
  80.2 3.1 %fusion.12 = (f32[16,64,1]{2,0,1:T(8,128)}, f32[16,64,1]{2,0,1:T(8,128)}, f32[16,64,1]{2,0,1:T(8,128)}, f32[16,64,1]{2,0,1:T(8,128)}, f32[16,64,1]{2,0,1:T(8,128...) fusion(f32[16,64,126]{2,0,1:T(8,128)S(1)} %get-tuple-element.455, ...), kind=kLoop, calls=%fused_computation.42 | loop fusion | flops 10240 | bytes 90112 | tf_op jit(solution)/shard_map/sub | solution.py:134
  83.3 1.4 %copy.26 = f32[16,64,1]{1,0,2:T(8,128)S(1)} copy(f32[16,64,1]{2,0,1:T(8,128)} %get-tuple-element.536) | data formatting | bytes 8192 | tf_op jit(solution)/shard_map/mul | solution.py:124
  84.8 1.3 copy.25
  86.2 1.3 copy.27
  87.6 1.3 copy.28
  88.9 1.3 copy.29
  91.5 31.2 %all_gather.7 = f32[4,16,1024]{2,0,1:T(4,128)S(1)} all-gather(f32[4,2,1024]{2,0,1:T(4,128)S(1)} %copy.40), channel_id=1, replica_groups=mesh['gx'=4,'gy'=8] {'gy'}, dimensions={1}, use_global_device_ids=true | all-gather | bytes 294912 | tf_op jit(solution)/shard_map/all_gather | solution.py:84
  122.7 4.9 %while.70 = (s32[]{:T(128)}, f32[1024]{0:T(1024)S(1)}, f32[1024]{0:T(1024)S(1)}, f32[16,1024]{1,0:T(8,128)S(1)}, f32[16,1024]{1,0:T(8,128)S(1)}, /*index=5*/f32[...) while((s32[]{:T(128)}, f32[1024]{0:T(1024)S(1)}, ...), condition=%wide.region_5.6_spmd.clone, body=%wide.region_4.5_spmd.clone.sunk | while | flops 8198 | bytes 82099 | solution.py:69
  127.6 2.8 %while.71 = (s32[]{:T(128)}, f32[1024]{0:T(1024)S(1)}, f32[16,1024]{1,0:T(8,128)S(1)}, f32[16,1024]{1,0:T(8,128)S(1)}, f32[16,1024]{1,0:T(8,128)S(1)}, /*index=5*/s32[]{:T(128)}, s32[]{:T(128)}, s32[]{:T(128)}) while((s32[]{:T(128)}, f32[1024]{0:T(1024)S(1)}, f32[16,1024]{1,0:T(8,128)S(1)}, f32[16,1024]{1,0:T(8,128)S(1)}, ...), condition=%wide.region_7.8_spmd.clone, body=%wide.region_6.7_spmd.clone.sunk | while | flops 3076 | bytes 41075 | solution.py:75
  130.9 0.7 fusion.36
  133.4 1.0 copy.45
  (310 shorter events, 33.6 us)
Async XLA Ops:
  0.0 5.6 %copy-start.5 = (f32[16,64,128]{2,1,0:T(8,128)S(1)}, f32[16,64,128]{2,1,0:T(8,128)}, u32[]{:S(2)}) copy-start(f32[16,64,128]{2,1,0:T(8,128)} %param.13) | copy-start | bytes 1572868
  1.9 21.1 %collective-permute-start.2 = (f32[2,16,1,128]{3,1,2,0:T(8,128)S(1)}, f32[2,16,1,128]{3,1,2,0:T(8,128)S(1)}, u32[]{:S(2)}, u32[]{:S(2)}) collective-permute-start(f32[2,16,1,128]{3,1,2,0:T(8,128)S(1)} %get-tuple-element.513), channel_id=1, source_target_pairs={{0,8},{8,16},{16,24},{1,9},{9,17},{17,25},{2,10},{10,18},{18,26},{... | collective-permute-start | bytes 49160 | tf_op jit(solution)/shard_map/ppermute | solution.py:15
  4.2 18.7 %collective-permute-start.3 = (f32[2,16,1,128]{3,1,2,0:T(8,128)S(1)}, f32[2,16,1,128]{3,1,2,0:T(8,128)S(1)}, u32[]{:S(2)}, u32[]{:S(2)}) collective-permute-start(f32[2,16,1,128]{3,1,2,0:T(8,128)S(1)} %get-tuple-element.514), channel_id=1, source_target_pairs={{8,0},{16,8},{24,16},{9,1},{17,9},{25,17},{10,2},{18,10},{26,18},{... | collective-permute-start | bytes 49160 | tf_op jit(solution)/shard_map/ppermute | solution.py:17
  8.9 6.1 %collective-permute-start = (f32[2,16,64,1]{2,1,3,0:T(8,128)S(1)}, f32[2,16,64,1]{2,1,3,0:T(8,128)S(1)}, u32[]{:S(2)}, u32[]{:S(2)}) collective-permute-start(f32[2,16,64,1]{2,1,3,0:T(8,128)S(1)} %copy.21), channel_id=1, source_target_pairs={{0,1},{1,2},{2,3},{3,4},{4,5},{5,6},{6,7},{8,9},{9,10},{10,11},{11... | collective-permute-start | bytes 24584 | tf_op jit(solution)/shard_map/ppermute | solution.py:15
  13.6 5.6 %collective-permute-start.1 = (f32[2,16,64,1]{2,1,3,0:T(8,128)S(1)}, f32[2,16,64,1]{2,1,3,0:T(8,128)S(1)}, u32[]{:S(2)}, u32[]{:S(2)}) collective-permute-start(f32[2,16,64,1]{2,1,3,0:T(8,128)S(1)} %copy.22), channel_id=1, source_target_pairs={{1,0},{2,1},{3,2},{4,3},{5,4},{6,5},{7,6},{9,8},{10,9},{11,10},{12... | collective-permute-start | bytes 24584 | tf_op jit(solution)/shard_map/ppermute | solution.py:17
  23.1 1.0 copy-start.4
  64.3 1.0 copy-start
  83.3 7.0 %copy-start.3 = (f32[16,64,1]{2,0,1:T(8,128)S(1)}, f32[16,64,1]{2,0,1:T(8,128)}, u32[]{:S(2)}) copy-start(f32[16,64,1]{2,0,1:T(8,128)} %get-tuple-element.559) | copy-start | bytes 12292
  83.3 7.3 %copy-start.2 = (f32[16,64,1]{2,0,1:T(8,128)S(1)}, f32[16,64,1]{2,0,1:T(8,128)}, u32[]{:S(2)}) copy-start(f32[16,64,1]{2,0,1:T(8,128)} %get-tuple-element.508) | copy-start | bytes 12292
  83.3 7.7 %copy-start.1 = (f32[16,64,1]{2,0,1:T(8,128)S(1)}, f32[16,64,1]{2,0,1:T(8,128)}, u32[]{:S(2)}) copy-start(f32[16,64,1]{2,0,1:T(8,128)} %get-tuple-element.509) | copy-start | bytes 12292
where the time goes:
time: 136 us; the launch traced here: 134 us
  local copies, waits for them, and re-layouts  57.1 us (42%)
  blocking collectives  39.5 us (29%)
  other arithmetic  21.9 us (16%)
  starting transfers between devices  9.17 us (7%)
  waiting for transfers between devices  3.69 us (3%)
  loops' own time  2.26 us (2%)
    all_gather x1, blocking collectives, interface_y(): lax.all_gather(rows, 'gy', axis=1, tiled=True)  31.2 us
    dynamic_update_slice x72, local copies, waits for them, and re-layouts, gathered_solve(): final, (ratios, values) = lax.scan(forward, (zeros, zeros), sequence)  20.2 us
    div x23, other arithmetic, reduce_lines(): (entry - lower * neighbor(entry, -stride, axis) - upper * neighbor(entry,...  11 us
    all_gather x1, blocking collectives, interface_x(): lax.all_gather(rows, 'gx', axis=1, tiled=True)  8.28 us
    dynamic_slice x24, local copies, waits for them, and re-layouts, gathered_solve(): final, solved = lax.scan(backward, zeros, (ratios, values), reverse=True)  7.1 us
    slice x52, local copies, waits for them, and re-layouts, neighbor(): part = lax.slice_in_dim(values, 0, length + step, axis=axis)  6.99 us
    ppermute x2, starting transfers between devices, padded(): lax.ppermute(tail, axis, [(i, (i + 1) % count) for i in range(ends)])  6.6 us
    ppermute x2, waiting for transfers between devices, padded(): lax.ppermute(head, axis, [((i + 1) % count, i) for i in range(ends)])  3.68 us
  transfers between devices with their start and end apart: 4, of which 1 were waited for; matrix products, arithmetic and copies ran while one was open for 6% of the time, Pallas kernels for 0%

commit v1 on v0

v1 whole, which is shorter than its diff:
```python
import functools

import jax
import jax.numpy as jnp
from jax import lax
from jax.experimental import pallas as pl
from jax.experimental.pallas import tpu as pltpu
from jax.sharding import PartitionSpec as P

MESH = pl.DeviceIdType.MESH
F32 = jnp.float32
SUB = 8


def recip(p):
    r = pl.reciprocal(p, approx=True)
    r = r * (2.0 - p * r)
    return r * (2.0 - p * r)


def factor_cells(face, coef):
    s = jnp.ones_like(face(0))
    to_p = face(0)
    at_p = jnp.zeros_like(s)
    for t in range(SUB - 1):
        right = face(t + 1)
        r = recip(s + to_p + right)
        a = right * r
        b = to_p * r
        coef[0, t] = r
        coef[1, t] = a
        coef[2, t] = b
        at_p = at_p + s * b
        s = 1.0 + s * a
        to_p = to_p * a
    return at_p, to_p, s


def halves(v):
    v = v.reshape((v.shape[0] // 2, 2) + v.shape[1:])
    return v[:, 0], v[:, 1]


def factor_tree(at_p, series, at_l, tree):
    level = 0
    at = 0
    while at_p.shape[0] > 1:
        pa, pb = halves(at_p)
        ga, gb = halves(series)
        la, lb = halves(at_l)
        c = la + pb
        r = recip(c + ga + gb)
        a = gb * r
        b = ga * r
        m = r.shape[0]
        tree[0, at : at + m] = r
        tree[1, at : at + m] = a
        tree[2, at : at + m] = b
        at_p = pa + c * b
        at_l = lb + c * a
        series = ga * a
        at += m
        level += 1
    return at_p[0], series[0], at_l[0]


def down_cells(source, coef, kept):
    d = source(0)
    at_p = None
    for t in range(SUB - 1):
        kept[t] = d
        share = coef[2, t] * d
        at_p = share if at_p is None else at_p + share
        d = source(t + 1) + coef[1, t] * d
    return at_p, d


def down_tree(at_p, at_l, tree, kept):
    at = 0
    while at_p.shape[0] > 1:
        pa, pb = halves(at_p)
        la, lb = halves(at_l)
        d = la + pb
        m = d.shape[0]
        kept[at : at + m] = d
        at_p = pa + tree[2, at : at + m] * d
        at_l = lb + tree[1, at : at + m] * d
        at += m
    return at_p[0], at_l[0]


def up_tree(u_p, u_l, tree, kept):
    nodes = u_l[None]
    total = kept.shape[0]
    m = 1
    at = total - 1
    while at >= 0:
        before = u_p[None] if m == 1 else jnp.concatenate([u_p[None], nodes[:-1]], axis=0)
        mid = (
            tree[0, at : at + m] * kept[at : at + m]
            + tree[1, at : at + m] * nodes
            + tree[2, at : at + m] * before
        )
        nodes = jnp.stack([mid, nodes], axis=1).reshape((2 * m,) + nodes.shape[1:])
        m *= 2
        at -= m
    before = jnp.concatenate([u_p[None], nodes[:-1]], axis=0)
    return before, nodes


def up_cells(before, nodes, coef, kept, put):
    u = nodes
    put(SUB - 1, u)
    for t in range(SUB - 2, -1, -1):
        u = coef[0, t] * kept[t] + coef[1, t] * u + coef[2, t] * before
        put(t, u)


def line_weights(me, n, every, weights, mine):
    zero = jnp.zeros(every.shape[2:], F32)
    ahead = []
    prior = None
    for j in range(n):
        p, g, l = every[j, 0], every[j, 1], every[j, 2]
        if prior is None:
            ahead.append((zero, zero, l + g))
            prior = l + g
        else:
            c = prior + p
            ratio = g * recip(c + g)
            now = l + c * ratio
            ahead.append((ratio, prior, now))
            prior = now
    back = [None] * n
    later = zero
    for j in range(n - 1, -1, -1):
        p, g, l = every[j, 0], every[j, 1], every[j, 2]
        c = later + l
        ratio = g * recip(c + g)
        now = p + c * ratio
        back[j] = (ratio, later, now)
        later = now
    own = [zero] * 6
    for j in range(n):
        here = me == j
        own = [jnp.where(here, v, o) for v, o in zip(ahead[j] + back[j], own)]
    rho, sf_prior, sf_now, tau, sb_later, sb_now = own
    inv_l = recip(sf_now + sb_later)
    inv_p = jnp.where(me > 0, recip(sf_prior + sb_now), zero)
    w_p = inv_p
    w_l = inv_l * rho
    for j in range(n - 1, -1, -1):
        left = me > j
        weights[j, 0] = jnp.where(left, w_p, zero)
        weights[j, 1] = jnp.where(left, w_l, zero)
        w_p = jnp.where(left, w_p * ahead[j][0], w_p)
        w_l = jnp.where(left, w_l * ahead[j][0], w_l)
    w_p = inv_p * tau
    w_l = inv_l
    for j in range(n):
        right = me < j
        weights[j, 0] = jnp.where(right, w_p, weights[j, 0])
        weights[j, 1] = jnp.where(right, w_l, weights[j, 1])
        w_p = jnp.where(right, w_p * back[j][0], w_p)
        w_l = jnp.where(right, w_l * back[j][0], w_l)
    mine[0] = rho
    mine[1] = tau
    mine[2] = inv_p
    mine[3] = inv_l


class Line:
    def __init__(self, axis, n, me, send, recv):
        self.axis, self.n, self.me, self.send, self.recv = axis, n, me, send, recv

    def copy(self, src, dst, slot, target):
        return pltpu.make_async_remote_copy(
            src_ref=src,
            dst_ref=dst,
            send_sem=self.send.at[slot],
            recv_sem=self.recv.at[slot],
            device_id={self.axis: target},
            device_id_type=MESH,
        )

    def others(self):
        for o in range(1, self.n):
            yield o, lax.rem(self.me + o, self.n), lax.rem(self.me + self.n - o, self.n)

    def start_all(self, src_of, buf, base):
        for o, target, _ in self.others():
            self.copy(src_of(o), buf.at[self.me], base + o - 1, target).start()

    def await_one(self, o, src, buf, base):
        source = lax.rem(self.me + self.n - o, self.n)
        self.copy(src, buf.at[source], base + o - 1, source).wait_recv()

    def done_sending(self, src_of, buf, base):
        for o, target, _ in self.others():
            self.copy(src_of(o), buf.at[self.me], base + o - 1, target).wait_send()


def share_coefs(line, mine, every):
    for i, v in enumerate(mine):
        every[line.me, i] = v
    line.start_all(lambda o: every.at[line.me], every, 0)


def await_coefs(line, every):
    for o, _, _ in line.others():
        line.await_one(o, every.at[line.me], every, 0)


def kernel(
    nx, ny, dims,
    u_hbm, kx_hbm, ky_hbm, out_ref,
    u_raw, kx_raw, ky_raw,
    u_x, gx, vx, turned, u_y, k_y,
    coef_x, kept_x, tree_x, tkept_x, every_x, weights_x, mine_x, out_x, got_x,
    coef_y, kept_y, tree_y, tkept_y, every_y, weights_y, mine_y, out_y, got_y,
    edge_x_out, edge_x_in, edge_y_out, edge_y_in,
    local_sem, xs, xr, ys, yr,
):
    nz, lx, ly = dims
    per = 128 // nz
    groups = lx // per
    ix = lax.axis_index("gx")
    iy = lax.axis_index("gy")
    loads = []
    for i, (src, dst) in enumerate(((ky_hbm, ky_raw), (u_hbm, u_raw), (kx_hbm, kx_raw))):
        cp = pltpu.make_async_copy(src, dst, local_sem.at[i])
        cp.start()
        loads.append(cp)
    line_x = Line("gx", nx, ix, xs, xr)
    line_y = Line("gy", ny, iy, ys, yr)
    barrier = pltpu.get_barrier_semaphore()
    for line in (line_x, line_y):
        for _, target, _ in line.others():
            pl.semaphore_signal(barrier, inc=1, device_id={line.axis: target}, device_id_type=MESH)

    def turn_in(block, g):
        turned[g * ly : (g + 1) * ly] = block.T

    def turned_row(y):
        return turned[pl.ds(y, groups, stride=ly), :]

    loads[0].wait()
    for g in range(groups):
        turn_in(jnp.concatenate([ky_raw[pl.ds(x, nz, stride=lx), :] for x in range(g * per, (g + 1) * per)], axis=0), g)
    for y in range(ly):
        k_y[y] = turned_row(y)
    loads[1].wait()
    for g in range(groups):
        rows = []
        for x in range(g * per, (g + 1) * per):
            row = u_raw[pl.ds(x, nz, stride=lx), :]
            u_x[x] = row
            rows.append(row)
        turn_in(jnp.concatenate(rows, axis=0), g)
    for y in range(ly):
        u_y[y] = turned_row(y)
    edge_y_out[0, 0] = k_y[0]
    edge_y_out[0, 1] = u_y[0]
    edge_y_out[1, 0] = k_y[ly - 1]
    edge_y_out[1, 1] = u_y[ly - 1]
    loads[2].wait()
    kx_last = kx_raw[pl.ds(lx - 1, nz, stride=lx), :]
    edge_x_out[...] = kx_last
    total = nx - 1 + ny - 1
    pl.semaphore_wait(barrier, total)

    hx = 2 * (nx - 1)
    hy = 2 * (ny - 1)

    def edge_x():
        return line_x.copy(edge_x_out, edge_x_in, hx, jnp.minimum(ix + 1, nx - 1))

    def edge_y_right():
        return line_y.copy(edge_y_out.at[1], edge_y_in.at[0], hy, jnp.minimum(iy + 1, ny - 1))

    def edge_y_left():
        return line_y.copy(edge_y_out.at[0], edge_y_in.at[1], hy + 1, jnp.maximum(iy - 1, 0))

    @pl.when(ix < nx - 1)
    def _():
        edge_x().start()

    @pl.when(iy < ny - 1)
    def _():
        edge_y_right().start()

    @pl.when(iy > 0)
    def _():
        edge_y_left().start()

    prior = kx_raw[pl.ds(0, nz, stride=lx), :]
    for x in range(1, lx):
        now = kx_raw[pl.ds(x, nz, stride=lx), :]
        gx[x // SUB, x % SUB] = 0.5 * (prior + now)
        prior = now

    @pl.when(ix > 0)
    def _():
        edge_x().wait_recv()

    gx[0, 0] = 0.5 * (jnp.where(ix > 0, edge_x_in[...], 0.0) + kx_raw[pl.ds(0, nz, stride=lx), :])
    at_p, series, at_l = factor_tree(*factor_cells(lambda t: gx[:, t], coef_x), tree_x)
    at_l = at_l + jnp.where(ix == nx - 1, 0.5 * kx_last, 0.0)
    share_coefs(line_x, (at_p, series, at_l), every_x)

    @pl.when(iy > 0)
    def _():
        edge_y_right().wait_recv()

    @pl.when(iy < ny - 1)
    def _():
        edge_y_left().wait_recv()

    k_prior = jnp.where(iy > 0, edge_y_in[0, 0], 0.0)
    u_prior = jnp.where(iy > 0, edge_y_in[0, 1], 0.0)
    k_last = k_y[ly - 1]
    k_now = k_y[0]
    u_now = u_y[0]
    face = 0.5 * (k_prior + k_now)
    k_y[0] = face
    flux = face * (u_now - u_prior)
    for y in range(ly):
        if y < ly - 1:
            k_next = k_y[y + 1]
            u_next = u_y[y + 1]
        else:
            k_next = jnp.where(iy < ny - 1, edge_y_in[1, 0], 0.0)
            u_next = jnp.where(iy < ny - 1, edge_y_in[1, 1], 0.0)
        face = 0.5 * (k_now + k_next)
        if y < ly - 1:
            k_y[y + 1] = face
        flux_next = face * (u_next - u_now)
        turned[pl.ds(y, groups, stride=ly), :] = u_now + (flux_next - flux)
        k_now, u_now, flux = k_next, u_next, flux_next
    for g in range(groups):
        back = turned[g * ly : (g + 1) * ly].T
        vx[g * per : (g + 1) * per] = back.reshape(per, nz, ly)
    vx_t = vx.reshape(lx // SUB, SUB, nz, ly)
    k_yt = k_y.reshape(ly // SUB, SUB, groups, 128)
    d_p, d_l = down_cells(lambda t: vx_t[:, t], coef_x, kept_x)
    d_p, d_l = down_tree(d_p, d_l, tree_x, tkept_x)
    await_coefs(line_x, every_x)
    line_weights(ix, nx, every_x, weights_x, mine_x)
    u_p, u_l = solve_ports_start(line_x, d_p, d_l, out_x, got_x, mine_x)

    at_p, series, at_l = factor_tree(*factor_cells(lambda t: k_yt[:, t], coef_y), tree_y)
    at_l = at_l + jnp.where(iy == ny - 1, 0.5 * k_last, 0.0)
    share_coefs(line_y, (at_p, series, at_l), every_y)

    u_p, u_l = solve_ports_end(line_x, u_p, u_l, out_x, got_x, weights_x)
    before, nodes = up_tree(u_p, u_l, tree_x, tkept_x)

    def put_x(t, v):
        vx_t[:, t] = v

    up_cells(before, nodes, coef_x, kept_x, put_x)
    for g in range(groups):
        q = vx[g * per : (g + 1) * per] - u_x[g * per : (g + 1) * per]
        turn_in(q.reshape(128, ly), g)
    for y in range(ly):
        u_y[y] = turned_row(y)
    u_yt = u_y.reshape(ly // SUB, SUB, groups, 128)
    d_p, d_l = down_cells(lambda t: u_yt[:, t], coef_y, kept_y)
    d_p, d_l = down_tree(d_p, d_l, tree_y, tkept_y)
    await_coefs(line_y, every_y)
    line_weights(iy, ny, every_y, weights_y, mine_y)
    u_p, u_l = solve_ports_start(line_y, d_p, d_l, out_y, got_y, mine_y)
    u_p, u_l = solve_ports_end(line_y, u_p, u_l, out_y, got_y, weights_y)
    before, nodes = up_tree(u_p, u_l, tree_y, tkept_y)

    def put_y(t, v):
        u_yt[:, t] = v

    up_cells(before, nodes, coef_y, kept_y, put_y)
    for y in range(ly):
        turned[pl.ds(y, groups, stride=ly), :] = u_y[y]
    for g in range(groups):
        w = turned[g * ly : (g + 1) * ly].T.reshape(per, nz, ly)
        o = u_x[g * per : (g + 1) * per] + 2.0 * w
        for i in range(per):
            out_ref[pl.ds(g * per + i, nz, stride=lx), :] = o[i]

    for line, every, out, got in ((line_x, every_x, out_x, got_x), (line_y, every_y, out_y, got_y)):
        line.done_sending(lambda o: every.at[line.me], every, 0)
        line.done_sending(lambda o: out.at[0], got, line.n - 1)

    @pl.when(ix < nx - 1)
    def _():
        edge_x().wait_send()

    @pl.when(iy < ny - 1)
    def _():
        edge_y_right().wait_send()

    @pl.when(iy > 0)
    def _():
        edge_y_left().wait_send()


def solve_ports_start(line, at_p, at_l, out, got, mine):
    n, me = line.n, line.me
    to_right = at_l + mine[0] * at_p
    to_left = at_p + mine[1] * at_l
    out[0] = to_right
    out[1] = to_left
    line.start_all(lambda o: out.at[(me + o) // n], got, n - 1)
    return mine[2] * to_left, mine[3] * to_right


def solve_ports_end(line, u_p, u_l, out, got, weights):
    for o, _, source in line.others():
        line.await_one(o, out.at[0], got, line.n - 1)
        v = got[source]
        u_p = u_p + weights[source, 0] * v
        u_l = u_l + weights[source, 1] * v
    return u_p, u_l


def on_device(nx, ny, state, kappa_x, kappa_y):
    nz, lx, ly = state.shape
    groups = nz * lx // 128
    flat = (nz * lx, ly)
    bx, by = lx // SUB, ly // SUB

    def line_scratch(n, blocks, rows):
        one = (rows, 128)
        return [
            pltpu.VMEM((3, SUB - 1, blocks) + one, F32),
            pltpu.VMEM((SUB - 1, blocks) + one, F32),
            pltpu.VMEM((3, blocks - 1) + one, F32),
            pltpu.VMEM((blocks - 1,) + one, F32),
            pltpu.VMEM((n, 3) + one, F32),
            pltpu.VMEM((n, 2) + one, F32),
            pltpu.VMEM((4,) + one, F32),
            pltpu.VMEM((2,) + one, F32),
            pltpu.VMEM((n,) + one, F32),
        ]

    scratch = (
        [pltpu.VMEM(flat, F32)] * 3
        + [
            pltpu.VMEM((lx, nz, ly), F32),
            pltpu.VMEM((bx, SUB, nz, ly), F32),
            pltpu.VMEM((lx, nz, ly), F32),
            pltpu.VMEM((groups * ly, 128), F32),
            pltpu.VMEM((ly, groups, 128), F32),
            pltpu.VMEM((ly, groups, 128), F32),
        ]
        + line_scratch(nx, bx, nz)
        + line_scratch(ny, by, groups)
        + [
            pltpu.VMEM((nz, ly), F32),
            pltpu.VMEM((nz, ly), F32),
            pltpu.VMEM((2, 2, groups, 128), F32),
            pltpu.VMEM((2, 2, groups, 128), F32),
            pltpu.SemaphoreType.DMA((3,)),
            pltpu.SemaphoreType.DMA((2 * nx - 1,)),
            pltpu.SemaphoreType.DMA((2 * nx - 1,)),
            pltpu.SemaphoreType.DMA((2 * ny,)),
            pltpu.SemaphoreType.DMA((2 * ny,)),
        ]
    )
    out = pl.pallas_call(
        functools.partial(kernel, nx, ny, (nz, lx, ly)),
        out_shape=jax.ShapeDtypeStruct(flat, F32),
        in_specs=[pl.BlockSpec(memory_space=pl.ANY)] * 3,
        out_specs=pl.BlockSpec(memory_space=pltpu.VMEM),
        scratch_shapes=scratch,
        compiler_params=pltpu.CompilerParams(
            collective_id=0, has_side_effects=True, vmem_limit_bytes=32 * 1024 * 1024
        ),
    )(state.reshape(flat), kappa_x.reshape(flat), kappa_y.reshape(flat))
    return out.reshape(state.shape)


def solution(mesh):
    spec = P(None, "gx", "gy")
    return jax.shard_map(
        functools.partial(on_device, mesh.shape["gx"], mesh.shape["gy"]),
        mesh=mesh,
        in_specs=(spec, spec, spec),
        out_specs=spec,
        check_vma=False,
    )
```

time: 136 us -> 25.8 us (0.19); the launches traced: 134 us -> 25.6 us
  local copies, waits for them, and re-layouts: 57.1 us -> 3.92 us
  blocking collectives: 39.5 us -> 0 us
  other arithmetic: 21.9 us -> 0 us
  Pallas kernels: 0 us -> 21.6 us
  starting transfers between devices: 9.17 us -> 0 us
  waiting for transfers between devices: 3.69 us -> 0 us
  loops' own time: 2.26 us -> 0 us
    all_gather x2 -> x0, blocking collectives: 39.5 us -> none  [the longest x1 31.2 us: interface_y(): lax.all_gather(rows, 'gy', axis=1, tiled=True)]
    pallas_call x0 -> x1, Pallas kernels: none -> 21.6 us  [on_device(): pl.pallas_call(functools.partial(kernel, nx, ny, (nz, lx, ly)), out_shape...]
    dynamic_update_slice x72 -> x0, local copies, waits for them, and re-layouts: 20.2 us -> none  [gathered_solve(): final, (ratios, values) = lax.scan(forward, (zeros, zeros), sequence)]
    slice x95 -> x0, local copies, waits for them, and re-layouts: 14.3 us -> none  [the longest x52 6.99 us: neighbor(): part = lax.slice_in_dim(values, 0, length + step, axis=axis)]
    div x50 -> x0, other arithmetic: 12.5 us -> none  [the longest x23 11 us: reduce_lines(): (entry - lower * neighbor(entry, -stride, axis) - upper * neighbor(entry,...]
    ppermute x4 -> x0, starting transfers between devices: 9.17 us -> none  [the longest x2 6.6 us: padded(): lax.ppermute(tail, axis, [(i, (i + 1) % count) for i in range(ends)])]
    dynamic_slice x24 -> x0, local copies, waits for them, and re-layouts: 7.1 us -> none  [gathered_solve(): final, solved = lax.scan(backward, zeros, (ratios, values), reverse=True)]
    ppermute x4 -> x0, waiting for transfers between devices: 3.69 us -> none  [the longest x2 3.68 us: padded(): lax.ppermute(head, axis, [((i + 1) % count, i) for i in range(ends)])]
  transfers between devices with their start and end apart: 4 -> 0, of which waited for: 1 -> 0; matrix products, arithmetic and copies ran while one was open for 6% -> 0% of each run, Pallas kernels for 0% -> 0%
where the time goes in v1:
time: 25.8 us; the launch traced here: 25.6 us
  Pallas kernels  21.6 us (84%)
  local copies, waits for them, and re-layouts  3.92 us (15%)
    pallas_call x1, Pallas kernels, on_device(): pl.pallas_call(functools.partial(kernel, nx, ny, (nz, lx, ly)), out_shape...  21.6 us
    unnamed x7, local copies, waits for them, and re-layouts  3.92 us

profile of v1, /device:TPU:0, one launch (start us, length us, event | category | flops | bytes accessed | tf_op | source)
XLA Modules:
  0.0 25.6 jit_solution(1386370889528138061)
XLA Ops:
  0.0 0.0 copy-start
  0.0 1.0 %copy-done = f32[16,64,128]{2,1,0:T(8,128)S(1)} copy-done((f32[16,64,128]{2,1,0:T(8,128)S(1)}, f32[16,64,128]{2,1,0:T(8,128)}, u32[]{:S(2)}) %copy-start) | copy-done | bytes 524312
  1.0 0.0 copy-start.1
  1.0 1.0 %copy-done.1 = f32[16,64,128]{2,1,0:T(8,128)S(1)} copy-done((f32[16,64,128]{2,1,0:T(8,128)S(1)}, f32[16,64,128]{2,1,0:T(8,128)}, u32[]{:S(2)}) %copy-start.1) | copy-done | bytes 524312
  2.1 0.0 copy-start.2
  2.1 1.0 %copy-done.2 = f32[16,64,128]{2,1,0:T(8,128)S(1)} copy-done((f32[16,64,128]{2,1,0:T(8,128)S(1)}, f32[16,64,128]{2,1,0:T(8,128)}, u32[]{:S(2)}) %copy-start.2) | copy-done | bytes 524312
  3.1 21.6 %shard_map.37 = f32[1024,128]{1,0:T(8,128)S(1)} custom-call(f32[1024,128]{1,0:T(8,128)S(1)} %bitcast.5, f32[1024,128]{1,0:T(8,128)S(1)} %bitcast.6, f32[1024,128]{1,0:T(8,128)S(1)} %bitcast.7), custom_call_target="tpu_custom_call" | custom-call | tf_op jit(solution)/shard_map/pallas_call | solution.py:468
  24.8 0.8 %copy.5 = f32[16,64,128]{2,1,0:T(8,128)} copy(f32[16,64,128]{2,1,0:T(8,128)S(1)} %bitcast.4) | data formatting | bytes 1048576
Async XLA Ops:
  0.0 1.0 %copy-start = (f32[16,64,128]{2,1,0:T(8,128)S(1)}, f32[16,64,128]{2,1,0:T(8,128)}, u32[]{:S(2)}) copy-start(f32[16,64,128]{2,1,0:T(8,128)} %param.3) | copy-start | bytes 1572868
  1.0 1.0 %copy-start.1 = (f32[16,64,128]{2,1,0:T(8,128)S(1)}, f32[16,64,128]{2,1,0:T(8,128)}, u32[]{:S(2)}) copy-start(f32[16,64,128]{2,1,0:T(8,128)} %param.4) | copy-start | bytes 1572868
  2.1 1.0 %copy-start.2 = (f32[16,64,128]{2,1,0:T(8,128)S(1)}, f32[16,64,128]{2,1,0:T(8,128)}, u32[]{:S(2)}) copy-start(f32[16,64,128]{2,1,0:T(8,128)} %param.5) | copy-start | bytes 1572868

commit v2 on v1

--- a/solution.py
+++ b/solution.py
@@ -14,7 +14,6 @@
 
 def recip(p):
     r = pl.reciprocal(p, approx=True)
-    r = r * (2.0 - p * r)
     return r * (2.0 - p * r)
 
 
@@ -116,7 +115,7 @@
         put(t, u)
 
 
-def line_weights(me, n, every, weights, mine):
+def line_ratios(me, n, every, chain, mine):
     zero = jnp.zeros(every.shape[2:], F32)
     ahead = []
     prior = None
@@ -144,29 +143,32 @@
     for j in range(n):
         here = me == j
         own = [jnp.where(here, v, o) for v, o in zip(ahead[j] + back[j], own)]
-    rho, sf_prior, sf_now, tau, sb_later, sb_now = own
+        chain[j, 0] = ahead[j][0]
+        chain[j, 1] = back[j][0]
+    for i, v in enumerate(own):
+        mine[i] = v
+
+
+def line_weights(me, n, chain, mine, weights):
+    rho, sf_prior, sf_now, tau, sb_later, sb_now = [mine[i] for i in range(6)]
+    zero = jnp.zeros_like(rho)
     inv_l = recip(sf_now + sb_later)
     inv_p = jnp.where(me > 0, recip(sf_prior + sb_now), zero)
-    w_p = inv_p
-    w_l = inv_l * rho
+    ahead = [None] * n
+    w_p, w_l = inv_p, inv_l * rho
     for j in range(n - 1, -1, -1):
         left = me > j
-        weights[j, 0] = jnp.where(left, w_p, zero)
-        weights[j, 1] = jnp.where(left, w_l, zero)
-        w_p = jnp.where(left, w_p * ahead[j][0], w_p)
-        w_l = jnp.where(left, w_l * ahead[j][0], w_l)
-    w_p = inv_p * tau
-    w_l = inv_l
+        ahead[j] = (w_p, w_l)
+        w_p = jnp.where(left, w_p * chain[j, 0], w_p)
+        w_l = jnp.where(left, w_l * chain[j, 0], w_l)
+    w_p, w_l = inv_p * tau, inv_l
     for j in range(n):
-        right = me < j
-        weights[j, 0] = jnp.where(right, w_p, weights[j, 0])
-        weights[j, 1] = jnp.where(right, w_l, weights[j, 1])
-        w_p = jnp.where(right, w_p * back[j][0], w_p)
-        w_l = jnp.where(right, w_l * back[j][0], w_l)
-    mine[0] = rho
-    mine[1] = tau
-    mine[2] = inv_p
-    mine[3] = inv_l
+        left, right = me > j, me < j
+        weights[j, 0] = jnp.where(left, ahead[j][0], w_p)
+        weights[j, 1] = jnp.where(left, ahead[j][1], w_l)
+        w_p = jnp.where(right, w_p * chain[j, 1], w_p)
+        w_l = jnp.where(right, w_l * chain[j, 1], w_l)
+    return inv_p, inv_l
 
 
 class Line:
@@ -211,19 +213,37 @@
         line.await_one(o, every.at[line.me], every, 0)
 
 
+def send_values(line, at_p, at_l, out, got, mine):
+    me = line.me
+    out[0] = at_l + mine[0] * at_p
+    out[1] = at_p + mine[3] * at_l
+    line.start_all(lambda o: out.at[(me + o) // line.n], got, line.n - 1)
+
+
+def take_values(line, inverses, out, got, weights):
+    u_p = inverses[0] * out[1]
+    u_l = inverses[1] * out[0]
+    for o, _, source in line.others():
+        line.await_one(o, out.at[0], got, line.n - 1)
+        v = got[source]
+        u_p = u_p + weights[source, 0] * v
+        u_l = u_l + weights[source, 1] * v
+    return u_p, u_l
+
+
 def kernel(
     nx, ny, dims,
     u_hbm, kx_hbm, ky_hbm, out_ref,
-    u_raw, kx_raw, ky_raw,
-    u_x, gx, vx, turned, u_y, k_y,
-    coef_x, kept_x, tree_x, tkept_x, every_x, weights_x, mine_x, out_x, got_x,
-    coef_y, kept_y, tree_y, tkept_y, every_y, weights_y, mine_y, out_y, got_y,
+    u_raw, kx_raw, ky_raw, nat, turned, gx, gy,
+    coef_x, kept_x, tree_x, tkept_x, every_x, weights_x, chain_x, mine_x, out_x, got_x,
+    coef_y, kept_y, tree_y, tkept_y, every_y, weights_y, chain_y, mine_y, out_y, got_y,
     edge_x_out, edge_x_in, edge_y_out, edge_y_in,
     local_sem, xs, xr, ys, yr,
 ):
     nz, lx, ly = dims
-    per = 128 // nz
-    groups = lx // per
+    lanes = 128
+    groups = nz * lx // lanes
+    bx, by = lx // SUB, ly // SUB
     ix = lax.axis_index("gx")
     iy = lax.axis_index("gy")
     loads = []
@@ -238,36 +258,14 @@
         for _, target, _ in line.others():
             pl.semaphore_signal(barrier, inc=1, device_id={line.axis: target}, device_id_type=MESH)
 
-    def turn_in(block, g):
-        turned[g * ly : (g + 1) * ly] = block.T
-
-    def turned_row(y):
+    def group(ref, g):
+        return ref[g * lanes : (g + 1) * lanes]
+
+    def x_rows(ref, x):
+        return ref[pl.ds(x, nz, stride=lx), :]
+
+    def y_rows(y):
         return turned[pl.ds(y, groups, stride=ly), :]
-
-    loads[0].wait()
-    for g in range(groups):
-        turn_in(jnp.concatenate([ky_raw[pl.ds(x, nz, stride=lx), :] for x in range(g * per, (g + 1) * per)], axis=0), g)
-    for y in range(ly):
-        k_y[y] = turned_row(y)
-    loads[1].wait()
-    for g in range(groups):
-        rows = []
-        for x in range(g * per, (g + 1) * per):
-            row = u_raw[pl.ds(x, nz, stride=lx), :]
-            u_x[x] = row
-            rows.append(row)
-        turn_in(jnp.concatenate(rows, axis=0), g)
-    for y in range(ly):
-        u_y[y] = turned_row(y)
-    edge_y_out[0, 0] = k_y[0]
-    edge_y_out[0, 1] = u_y[0]
-    edge_y_out[1, 0] = k_y[ly - 1]
-    edge_y_out[1, 1] = u_y[ly - 1]
-    loads[2].wait()
-    kx_last = kx_raw[pl.ds(lx - 1, nz, stride=lx), :]
-    edge_x_out[...] = kx_last
-    total = nx - 1 + ny - 1
-    pl.semaphore_wait(barrier, total)
 
     hx = 2 * (nx - 1)
     hy = 2 * (ny - 1)
@@ -281,6 +279,24 @@
     def edge_y_left():
         return line_y.copy(edge_y_out.at[0], edge_y_in.at[1], hy + 1, jnp.maximum(iy - 1, 0))
 
+    row8 = lax.broadcasted_iota(jnp.int32, (8, ly), 0)
+    lane8 = lax.broadcasted_iota(jnp.int32, (8, ly), 1)
+    pick = jnp.where(((row8 == 0) & (lane8 == 0)) | ((row8 == 1) & (lane8 == ly - 1)), 1.0, 0.0).astype(F32)
+    for kind, (load, raw) in enumerate(((loads[0], ky_raw), (loads[1], u_raw))):
+        load.wait()
+        for g in range(groups):
+            edges = lax.dot_general(
+                pick, group(raw, g), (((1,), (1,)), ((), ())),
+                precision=lax.Precision.HIGHEST, preferred_element_type=F32,
+            )
+            edge_y_out[0, kind, g : g + 1] = edges[0:1]
+            edge_y_out[1, kind, g : g + 1] = edges[1:2]
+    loads[2].wait()
+    kx_first = x_rows(kx_raw, 0)
+    kx_last = x_rows(kx_raw, lx - 1)
+    edge_x_out[...] = kx_last
+    pl.semaphore_wait(barrier, nx - 1 + ny - 1)
+
     @pl.when(ix < nx - 1)
     def _():
         edge_x().start()
@@ -293,17 +309,25 @@
     def _():
         edge_y_left().start()
 
-    prior = kx_raw[pl.ds(0, nz, stride=lx), :]
+    prior = kx_first
     for x in range(1, lx):
-        now = kx_raw[pl.ds(x, nz, stride=lx), :]
+        now = x_rows(kx_raw, x)
         gx[x // SUB, x % SUB] = 0.5 * (prior + now)
         prior = now
+    for g in range(groups):
+        turned[g * ly : (g + 1) * ly] = group(ky_raw, g).T
+    prior = y_rows(0)
+    for y in range(1, ly):
+        now = y_rows(y)
+        gy[y // SUB, y % SUB] = 0.5 * (prior + now)
+        prior = now
+    ky_last = prior
 
     @pl.when(ix > 0)
     def _():
         edge_x().wait_recv()
 
-    gx[0, 0] = 0.5 * (jnp.where(ix > 0, edge_x_in[...], 0.0) + kx_raw[pl.ds(0, nz, stride=lx), :])
+    gx[0, 0] = 0.5 * (jnp.where(ix > 0, edge_x_in[...], 0.0) + kx_first)
     at_p, series, at_l = factor_tree(*factor_cells(lambda t: gx[:, t], coef_x), tree_x)
     at_l = at_l + jnp.where(ix == nx - 1, 0.5 * kx_last, 0.0)
     share_coefs(line_x, (at_p, series, at_l), every_x)
@@ -316,74 +340,71 @@
     def _():
         edge_y_left().wait_recv()
 
-    k_prior = jnp.where(iy > 0, edge_y_in[0, 0], 0.0)
-    u_prior = jnp.where(iy > 0, edge_y_in[0, 1], 0.0)
-    k_last = k_y[ly - 1]
-    k_now = k_y[0]
-    u_now = u_y[0]
-    face = 0.5 * (k_prior + k_now)
-    k_y[0] = face
-    flux = face * (u_now - u_prior)
-    for y in range(ly):
-        if y < ly - 1:
-            k_next = k_y[y + 1]
-            u_next = u_y[y + 1]
-        else:
-            k_next = jnp.where(iy < ny - 1, edge_y_in[1, 0], 0.0)
-            u_next = jnp.where(iy < ny - 1, edge_y_in[1, 1], 0.0)
-        face = 0.5 * (k_now + k_next)
-        if y < ly - 1:
-            k_y[y + 1] = face
-        flux_next = face * (u_next - u_now)
-        turned[pl.ds(y, groups, stride=ly), :] = u_now + (flux_next - flux)
-        k_now, u_now, flux = k_next, u_next, flux_next
+    k0, u0, k1, u1 = edge_y_out[0, 0], edge_y_out[0, 1], edge_y_out[1, 0], edge_y_out[1, 1]
+    inner, last = iy > 0, iy < ny - 1
+    face_0 = 0.5 * (jnp.where(inner, edge_y_in[0, 0], 0.0) + k0)
+    gy[0, 0] = face_0
+    face_1 = 0.5 * (jnp.where(last, edge_y_in[1, 0], 0.0) + k1)
+    flux_0 = face_0 * (jnp.where(inner, edge_y_in[0, 1], 0.0) - u0)
+    flux_1 = face_1 * (jnp.where(last, edge_y_in[1, 1], 0.0) - u1)
+    ends = jnp.concatenate([flux_0, flux_1], axis=0).T
+    row = lax.broadcasted_iota(jnp.int32, (2 * groups, ly), 0)
+    lane = lax.broadcasted_iota(jnp.int32, (2 * groups, ly), 1)
+    inside = lax.broadcasted_iota(jnp.int32, (lanes, ly), 1) > 0
     for g in range(groups):
-        back = turned[g * ly : (g + 1) * ly].T
-        vx[g * per : (g + 1) * per] = back.reshape(per, nz, ly)
-    vx_t = vx.reshape(lx // SUB, SUB, nz, ly)
-    k_yt = k_y.reshape(ly // SUB, SUB, groups, 128)
-    d_p, d_l = down_cells(lambda t: vx_t[:, t], coef_x, kept_x)
+        put = jnp.where(((row == g) & (lane == 0)) | ((row == groups + g) & (lane == ly - 1)), 1.0, 0.0).astype(F32)
+        added = lax.dot_general(
+            ends, put, (((1,), (0,)), ((), ())), precision=lax.Precision.HIGHEST, preferred_element_type=F32
+        )
+        u = group(u_raw, g)
+        k = group(ky_raw, g)
+        flux = jnp.where(inside, 0.5 * (k + pltpu.roll(k, 1, 1)) * (u - pltpu.roll(u, 1, 1)), 0.0)
+        nat[g * lanes : (g + 1) * lanes] = (u + added) + (pltpu.roll(flux, ly - 1, 1) - flux)
+
+    def x_cells(t):
+        return jnp.stack([x_rows(nat, b * SUB + t) for b in range(bx)], axis=0)
+
+    d_p, d_l = down_cells(x_cells, coef_x, kept_x)
     d_p, d_l = down_tree(d_p, d_l, tree_x, tkept_x)
     await_coefs(line_x, every_x)
-    line_weights(ix, nx, every_x, weights_x, mine_x)
-    u_p, u_l = solve_ports_start(line_x, d_p, d_l, out_x, got_x, mine_x)
-
-    at_p, series, at_l = factor_tree(*factor_cells(lambda t: k_yt[:, t], coef_y), tree_y)
-    at_l = at_l + jnp.where(iy == ny - 1, 0.5 * k_last, 0.0)
+    line_ratios(ix, nx, every_x, chain_x, mine_x)
+    send_values(line_x, d_p, d_l, out_x, got_x, mine_x)
+
+    inverses = line_weights(ix, nx, chain_x, mine_x, weights_x)
+    at_p, series, at_l = factor_tree(*factor_cells(lambda t: gy[:, t], coef_y), tree_y)
+    at_l = at_l + jnp.where(iy == ny - 1, 0.5 * ky_last, 0.0)
     share_coefs(line_y, (at_p, series, at_l), every_y)
 
-    u_p, u_l = solve_ports_end(line_x, u_p, u_l, out_x, got_x, weights_x)
+    u_p, u_l = take_values(line_x, inverses, out_x, got_x, weights_x)
     before, nodes = up_tree(u_p, u_l, tree_x, tkept_x)
 
     def put_x(t, v):
-        vx_t[:, t] = v
+        for b in range(bx):
+            nat[pl.ds(b * SUB + t, nz, stride=lx), :] = v[b]
 
     up_cells(before, nodes, coef_x, kept_x, put_x)
     for g in range(groups):
-        q = vx[g * per : (g + 1) * per] - u_x[g * per : (g + 1) * per]
-        turn_in(q.reshape(128, ly), g)
-    for y in range(ly):
-        u_y[y] = turned_row(y)
-    u_yt = u_y.reshape(ly // SUB, SUB, groups, 128)
-    d_p, d_l = down_cells(lambda t: u_yt[:, t], coef_y, kept_y)
+        turned[g * ly : (g + 1) * ly] = (group(nat, g) - group(u_raw, g)).T
+
+    def y_cells(t):
+        return jnp.stack([y_rows(b * SUB + t) for b in range(by)], axis=0)
+
+    d_p, d_l = down_cells(y_cells, coef_y, kept_y)
     d_p, d_l = down_tree(d_p, d_l, tree_y, tkept_y)
     await_coefs(line_y, every_y)
-    line_weights(iy, ny, every_y, weights_y, mine_y)
-    u_p, u_l = solve_ports_start(line_y, d_p, d_l, out_y, got_y, mine_y)
-    u_p, u_l = solve_ports_end(line_y, u_p, u_l, out_y, got_y, weights_y)
+    line_ratios(iy, ny, every_y, chain_y, mine_y)
+    send_values(line_y, d_p, d_l, out_y, got_y, mine_y)
+    inverses = line_weights(iy, ny, chain_y, mine_y, weights_y)
+    u_p, u_l = take_values(line_y, inverses, out_y, got_y, weights_y)
     before, nodes = up_tree(u_p, u_l, tree_y, tkept_y)
 
     def put_y(t, v):
-        u_yt[:, t] = v
+        for b in range(by):
+            turned[pl.ds(b * SUB + t, groups, stride=ly), :] = v[b]
 
     up_cells(before, nodes, coef_y, kept_y, put_y)
-    for y in range(ly):
-        turned[pl.ds(y, groups, stride=ly), :] = u_y[y]
     for g in range(groups):
-        w = turned[g * ly : (g + 1) * ly].T.reshape(per, nz, ly)
-        o = u_x[g * per : (g + 1) * per] + 2.0 * w
-        for i in range(per):
-            out_ref[pl.ds(g * per + i, nz, stride=lx), :] = o[i]
+        out_ref[g * lanes : (g + 1) * lanes] = group(u_raw, g) + 2.0 * turned[g * ly : (g + 1) * ly].T
 
     for line, every, out, got in ((line_x, every_x, out_x, got_x), (line_y, every_y, out_y, got_y)):
         line.done_sending(lambda o: every.at[line.me], every, 0)
@@ -400,25 +421,6 @@
     @pl.when(iy > 0)
     def _():
         edge_y_left().wait_send()
-
-
-def solve_ports_start(line, at_p, at_l, out, got, mine):
-    n, me = line.n, line.me
-    to_right = at_l + mine[0] * at_p
-    to_left = at_p + mine[1] * at_l
-    out[0] = to_right
-    out[1] = to_left
-    line.start_all(lambda o: out.at[(me + o) // n], got, n - 1)
-    return mine[2] * to_left, mine[3] * to_right
-
-
-def solve_ports_end(line, u_p, u_l, out, got, weights):
-    for o, _, source in line.others():
-        line.await_one(o, out.at[0], got, line.n - 1)
-        v = got[source]
-        u_p = u_p + weights[source, 0] * v
-        u_l = u_l + weights[source, 1] * v
-    return u_p, u_l
 
 
 def on_device(nx, ny, state, kappa_x, kappa_y):
@@ -436,20 +438,17 @@
             pltpu.VMEM((blocks - 1,) + one, F32),
             pltpu.VMEM((n, 3) + one, F32),
             pltpu.VMEM((n, 2) + one, F32),
-            pltpu.VMEM((4,) + one, F32),
+            pltpu.VMEM((n, 2) + one, F32),
+            pltpu.VMEM((6,) + one, F32),
             pltpu.VMEM((2,) + one, F32),
             pltpu.VMEM((n,) + one, F32),
         ]
 
     scratch = (
-        [pltpu.VMEM(flat, F32)] * 3
+        [pltpu.VMEM(flat, F32)] * 5
         + [
-            pltpu.VMEM((lx, nz, ly), F32),
             pltpu.VMEM((bx, SUB, nz, ly), F32),
-            pltpu.VMEM((lx, nz, ly), F32),
-            pltpu.VMEM((groups * ly, 128), F32),
-            pltpu.VMEM((ly, groups, 128), F32),
-            pltpu.VMEM((ly, groups, 128), F32),
+            pltpu.VMEM((by, SUB, groups, 128), F32),
         ]
         + line_scratch(nx, bx, nz)
         + line_scratch(ny, by, groups)
@@ -468,13 +467,13 @@
     out = pl.pallas_call(
         functools.partial(kernel, nx, ny, (nz, lx, ly)),
         out_shape=jax.ShapeDtypeStruct(flat, F32),
-        in_specs=[pl.BlockSpec(memory_space=pl.ANY)] * 3,
+        in_specs=[pl.BlockSpec(memory_space=pltpu.HBM)] * 3,
         out_specs=pl.BlockSpec(memory_space=pltpu.VMEM),
         scratch_shapes=scratch,
         compiler_params=pltpu.CompilerParams(
             collective_id=0, has_side_effects=True, vmem_limit_bytes=32 * 1024 * 1024
         ),
-    )(state.reshape(flat), kappa_x.reshape(flat), kappa_y.reshape(flat))
+    )(*[pltpu.with_memory_space_constraint(v.reshape(flat), pltpu.HBM) for v in (state, kappa_x, kappa_y)])
     return out.reshape(state.shape)
 
 

time: 25.8 us -> 22 us (0.85)
  local copies, waits for them, and re-layouts: 3.92 us -> 0.8 us
  Pallas kernels: 21.6 us -> 21 us
    unnamed x7 -> x1, local copies, waits for them, and re-layouts: 3.92 us -> 0.8 us
    pallas_call x1, Pallas kernels: 21.6 us -> 21 us  [on_device(): pl.pallas_call(functools.partial(kernel, nx, ny, (nz, lx, ly)), out_shape...]
where the time goes in v2:
time: 22 us; the launch traced here: 21.8 us
  Pallas kernels  21 us (95%)
  local copies, waits for them, and re-layouts  0.8 us (4%)
    pallas_call x1, Pallas kernels, on_device(): pl.pallas_call(functools.partial(kernel, nx, ny, (nz, lx, ly)), out_shape...  21 us
    unnamed x1, local copies, waits for them, and re-layouts  0.8 us

profile of v2, /device:TPU:0, one launch (start us, length us, event | category | flops | bytes accessed | tf_op | source)
XLA Modules:
  0.0 21.8 jit_solution(4363126087997823455)
XLA Ops:
  0.0 21.0 %shard_map.37 = f32[1024,128]{1,0:T(8,128)S(1)} custom-call(f32[1024,128]{1,0:T(8,128)} %bitcast.5, f32[1024,128]{1,0:T(8,128)} %bitcast.6, f32[1024,128]{1,0:T(8,128)} %bitcast.7), custom_call_target="tpu_custom_call" | custom-call | tf_op jit(solution)/shard_map/pallas_call | solution.py:467
  21.0 0.8 %copy.5 = f32[16,64,128]{2,1,0:T(8,128)} copy(f32[16,64,128]{2,1,0:T(8,128)S(1)} %bitcast.4) | data formatting | bytes 1048576

commit v3 on v2

--- a/solution.py
+++ b/solution.py
@@ -237,7 +237,7 @@
     u_raw, kx_raw, ky_raw, nat, turned, gx, gy,
     coef_x, kept_x, tree_x, tkept_x, every_x, weights_x, chain_x, mine_x, out_x, got_x,
     coef_y, kept_y, tree_y, tkept_y, every_y, weights_y, chain_y, mine_y, out_y, got_y,
-    edge_x_out, edge_x_in, edge_y_out, edge_y_in,
+    edge_x_in, edge_y_out, edge_y_in, ends,
     local_sem, xs, xr, ys, yr,
 ):
     nz, lx, ly = dims
@@ -271,7 +271,7 @@
     hy = 2 * (ny - 1)
 
     def edge_x():
-        return line_x.copy(edge_x_out, edge_x_in, hx, jnp.minimum(ix + 1, nx - 1))
+        return line_x.copy(kx_hbm.reshape(nz, lx, ly).at[:, lx - 1, :], edge_x_in, hx, jnp.minimum(ix + 1, nx - 1))
 
     def edge_y_right():
         return line_y.copy(edge_y_out.at[1], edge_y_in.at[0], hy, jnp.minimum(iy + 1, ny - 1))
@@ -279,41 +279,87 @@
     def edge_y_left():
         return line_y.copy(edge_y_out.at[0], edge_y_in.at[1], hy + 1, jnp.maximum(iy - 1, 0))
 
-    row8 = lax.broadcasted_iota(jnp.int32, (8, ly), 0)
-    lane8 = lax.broadcasted_iota(jnp.int32, (8, ly), 1)
-    pick = jnp.where(((row8 == 0) & (lane8 == 0)) | ((row8 == 1) & (lane8 == ly - 1)), 1.0, 0.0).astype(F32)
+    pl.semaphore_wait(barrier, nx - 1 + ny - 1)
+
+    @pl.when(ix < nx - 1)
+    def _():
+        edge_x().start()
+
+    lane = lax.broadcasted_iota(jnp.int32, (lanes, ly), 1)
+    packed = None
     for kind, (load, raw) in enumerate(((loads[0], ky_raw), (loads[1], u_raw))):
         load.wait()
         for g in range(groups):
-            edges = lax.dot_general(
-                pick, group(raw, g), (((1,), (1,)), ((), ())),
-                precision=lax.Precision.HIGHEST, preferred_element_type=F32,
-            )
-            edge_y_out[0, kind, g : g + 1] = edges[0:1]
-            edge_y_out[1, kind, g : g + 1] = edges[1:2]
+            at = 2 * (kind * groups + g)
+            moved = pltpu.roll(group(raw, g), at + 1, 1)
+            packed = moved if packed is None else jnp.where(lane >= at, moved, packed)
+    ends[...] = packed.T
+    for kind in range(2):
+        for side in range(2):
+            edge_y_out[side, kind] = ends[pl.ds(2 * kind * groups + 1 - side, groups, stride=2), :]
+
+    @pl.when(iy < ny - 1)
+    def _():
+        edge_y_right().start()
+
+    @pl.when(iy > 0)
+    def _():
+        edge_y_left().start()
+
     loads[2].wait()
     kx_first = x_rows(kx_raw, 0)
     kx_last = x_rows(kx_raw, lx - 1)
-    edge_x_out[...] = kx_last
-    pl.semaphore_wait(barrier, nx - 1 + ny - 1)
-
-    @pl.when(ix < nx - 1)
-    def _():
-        edge_x().start()
-
-    @pl.when(iy < ny - 1)
-    def _():
-        edge_y_right().start()
-
-    @pl.when(iy > 0)
-    def _():
-        edge_y_left().start()
-
     prior = kx_first
     for x in range(1, lx):
         now = x_rows(kx_raw, x)
         gx[x // SUB, x % SUB] = 0.5 * (prior + now)
         prior = now
+    @pl.when(ix > 0)
+    def _():
+        edge_x().wait_recv()
+
+    gx[0, 0] = 0.5 * (jnp.where(ix > 0, edge_x_in[...], 0.0) + kx_first)
+    at_p, series, at_l = factor_tree(*factor_cells(lambda t: gx[:, t], coef_x), tree_x)
+    at_l = at_l + jnp.where(ix == nx - 1, 0.5 * kx_last, 0.0)
+    share_coefs(line_x, (at_p, series, at_l), every_x)
+
+    @pl.when(iy > 0)
+    def _():
+        edge_y_right().wait_recv()
+
+    @pl.when(iy < ny - 1)
+    def _():
+        edge_y_left().wait_recv()
+
+    k0, u0, k1, u1 = edge_y_out[0, 0], edge_y_out[0, 1], edge_y_out[1, 0], edge_y_out[1, 1]
+    inner, last = iy > 0, iy < ny - 1
+    face_0 = 0.5 * (jnp.where(inner, edge_y_in[0, 0], 0.0) + k0)
+    gy[0, 0] = face_0
+    face_1 = 0.5 * (jnp.where(last, edge_y_in[1, 0], 0.0) + k1)
+    flux_0 = face_0 * (jnp.where(inner, edge_y_in[0, 1], 0.0) - u0)
+    flux_1 = face_1 * (jnp.where(last, edge_y_in[1, 1], 0.0) - u1)
+    ends[pl.ds(0, groups, stride=2), :] = flux_1
+    ends[pl.ds(1, groups, stride=2), :] = -flux_0
+    fluxes = ends[...].T
+    for g in range(groups):
+        outer = pltpu.roll(fluxes, (ly - 2 * g - 1) % ly, 1)
+        u = group(u_raw, g)
+        k = group(ky_raw, g)
+        flux = 0.5 * (k + pltpu.roll(k, 1, 1)) * (u - pltpu.roll(u, 1, 1))
+        flux = jnp.where(lane > 0, flux, outer)
+        later = jnp.where(lane < ly - 1, pltpu.roll(flux, ly - 1, 1), outer)
+        nat[g * lanes : (g + 1) * lanes] = u + (later - flux)
+
+    await_coefs(line_x, every_x)
+    def x_cells(t):
+        return jnp.stack([x_rows(nat, b * SUB + t) for b in range(bx)], axis=0)
+
+    d_p, d_l = down_cells(x_cells, coef_x, kept_x)
+    d_p, d_l = down_tree(d_p, d_l, tree_x, tkept_x)
+    line_ratios(ix, nx, every_x, chain_x, mine_x)
+    send_values(line_x, d_p, d_l, out_x, got_x, mine_x)
+
+    inverses = line_weights(ix, nx, chain_x, mine_x, weights_x)
     for g in range(groups):
         turned[g * ly : (g + 1) * ly] = group(ky_raw, g).T
     prior = y_rows(0)
@@ -322,55 +368,6 @@
         gy[y // SUB, y % SUB] = 0.5 * (prior + now)
         prior = now
     ky_last = prior
-
-    @pl.when(ix > 0)
-    def _():
-        edge_x().wait_recv()
-
-    gx[0, 0] = 0.5 * (jnp.where(ix > 0, edge_x_in[...], 0.0) + kx_first)
-    at_p, series, at_l = factor_tree(*factor_cells(lambda t: gx[:, t], coef_x), tree_x)
-    at_l = at_l + jnp.where(ix == nx - 1, 0.5 * kx_last, 0.0)
-    share_coefs(line_x, (at_p, series, at_l), every_x)
-
-    @pl.when(iy > 0)
-    def _():
-        edge_y_right().wait_recv()
-
-    @pl.when(iy < ny - 1)
-    def _():
-        edge_y_left().wait_recv()
-
-    k0, u0, k1, u1 = edge_y_out[0, 0], edge_y_out[0, 1], edge_y_out[1, 0], edge_y_out[1, 1]
-    inner, last = iy > 0, iy < ny - 1
-    face_0 = 0.5 * (jnp.where(inner, edge_y_in[0, 0], 0.0) + k0)
-    gy[0, 0] = face_0
-    face_1 = 0.5 * (jnp.where(last, edge_y_in[1, 0], 0.0) + k1)
-    flux_0 = face_0 * (jnp.where(inner, edge_y_in[0, 1], 0.0) - u0)
-    flux_1 = face_1 * (jnp.where(last, edge_y_in[1, 1], 0.0) - u1)
-    ends = jnp.concatenate([flux_0, flux_1], axis=0).T
-    row = lax.broadcasted_iota(jnp.int32, (2 * groups, ly), 0)
-    lane = lax.broadcasted_iota(jnp.int32, (2 * groups, ly), 1)
-    inside = lax.broadcasted_iota(jnp.int32, (lanes, ly), 1) > 0
-    for g in range(groups):
-        put = jnp.where(((row == g) & (lane == 0)) | ((row == groups + g) & (lane == ly - 1)), 1.0, 0.0).astype(F32)
-        added = lax.dot_general(
-            ends, put, (((1,), (0,)), ((), ())), precision=lax.Precision.HIGHEST, preferred_element_type=F32
-        )
-        u = group(u_raw, g)
-        k = group(ky_raw, g)
-        flux = jnp.where(inside, 0.5 * (k + pltpu.roll(k, 1, 1)) * (u - pltpu.roll(u, 1, 1)), 0.0)
-        nat[g * lanes : (g + 1) * lanes] = (u + added) + (pltpu.roll(flux, ly - 1, 1) - flux)
-
-    def x_cells(t):
-        return jnp.stack([x_rows(nat, b * SUB + t) for b in range(bx)], axis=0)
-
-    d_p, d_l = down_cells(x_cells, coef_x, kept_x)
-    d_p, d_l = down_tree(d_p, d_l, tree_x, tkept_x)
-    await_coefs(line_x, every_x)
-    line_ratios(ix, nx, every_x, chain_x, mine_x)
-    send_values(line_x, d_p, d_l, out_x, got_x, mine_x)
-
-    inverses = line_weights(ix, nx, chain_x, mine_x, weights_x)
     at_p, series, at_l = factor_tree(*factor_cells(lambda t: gy[:, t], coef_y), tree_y)
     at_l = at_l + jnp.where(iy == ny - 1, 0.5 * ky_last, 0.0)
     share_coefs(line_y, (at_p, series, at_l), every_y)
@@ -389,12 +386,28 @@
     def y_cells(t):
         return jnp.stack([y_rows(b * SUB + t) for b in range(by)], axis=0)
 
+    await_coefs(line_y, every_y)
     d_p, d_l = down_cells(y_cells, coef_y, kept_y)
     d_p, d_l = down_tree(d_p, d_l, tree_y, tkept_y)
-    await_coefs(line_y, every_y)
     line_ratios(iy, ny, every_y, chain_y, mine_y)
     send_values(line_y, d_p, d_l, out_y, got_y, mine_y)
     inverses = line_weights(iy, ny, chain_y, mine_y, weights_y)
+    line_x.done_sending(lambda o: every_x.at[ix], every_x, 0)
+    line_x.done_sending(lambda o: out_x.at[0], got_x, nx - 1)
+    line_y.done_sending(lambda o: every_y.at[iy], every_y, 0)
+
+    @pl.when(ix < nx - 1)
+    def _():
+        edge_x().wait_send()
+
+    @pl.when(iy < ny - 1)
+    def _():
+        edge_y_right().wait_send()
+
+    @pl.when(iy > 0)
+    def _():
+        edge_y_left().wait_send()
+
     u_p, u_l = take_values(line_y, inverses, out_y, got_y, weights_y)
     before, nodes = up_tree(u_p, u_l, tree_y, tkept_y)
 
@@ -406,21 +419,7 @@
     for g in range(groups):
         out_ref[g * lanes : (g + 1) * lanes] = group(u_raw, g) + 2.0 * turned[g * ly : (g + 1) * ly].T
 
-    for line, every, out, got in ((line_x, every_x, out_x, got_x), (line_y, every_y, out_y, got_y)):
-        line.done_sending(lambda o: every.at[line.me], every, 0)
-        line.done_sending(lambda o: out.at[0], got, line.n - 1)
-
-    @pl.when(ix < nx - 1)
-    def _():
-        edge_x().wait_send()
-
-    @pl.when(iy < ny - 1)
-    def _():
-        edge_y_right().wait_send()
-
-    @pl.when(iy > 0)
-    def _():
-        edge_y_left().wait_send()
+    line_y.done_sending(lambda o: out_y.at[0], got_y, ny - 1)
 
 
 def on_device(nx, ny, state, kappa_x, kappa_y):
@@ -454,9 +453,9 @@
         + line_scratch(ny, by, groups)
         + [
             pltpu.VMEM((nz, ly), F32),
-            pltpu.VMEM((nz, ly), F32),
             pltpu.VMEM((2, 2, groups, 128), F32),
             pltpu.VMEM((2, 2, groups, 128), F32),
+            pltpu.VMEM((128, 128), F32),
             pltpu.SemaphoreType.DMA((3,)),
             pltpu.SemaphoreType.DMA((2 * nx - 1,)),
             pltpu.SemaphoreType.DMA((2 * nx - 1,)),

time: 22 us -> 23.3 us (1.059)
  Pallas kernels: 21 us -> 22.3 us
    pallas_call x1, Pallas kernels: 21 us -> 22.3 us  [on_device(): pl.pallas_call(functools.partial(kernel, nx, ny, (nz, lx, ly)), out_shape...]
where the time goes in v3:
time: 23.3 us; the launch traced here: 23.1 us
  Pallas kernels  22.3 us (96%)
  local copies, waits for them, and re-layouts  0.8 us (3%)
    pallas_call x1, Pallas kernels, on_device(): pl.pallas_call(functools.partial(kernel, nx, ny, (nz, lx, ly)), out_shape...  22.3 us
    unnamed x1, local copies, waits for them, and re-layouts  0.8 us

profile of v3, /device:TPU:0, one launch (start us, length us, event | category | flops | bytes accessed | tf_op | source)
XLA Modules:
  0.0 23.1 jit_solution(3108286503985758629)
XLA Ops:
  0.0 22.3 %shard_map.37 = f32[1024,128]{1,0:T(8,128)S(1)} custom-call(f32[1024,128]{1,0:T(8,128)} %bitcast.5, f32[1024,128]{1,0:T(8,128)} %bitcast.6, f32[1024,128]{1,0:T(8,128)} %bitcast.7), custom_call_target="tpu_custom_call" | custom-call | tf_op jit(solution)/shard_map/pallas_call | solution.py:466
  22.3 0.8 %copy.5 = f32[16,64,128]{2,1,0:T(8,128)} copy(f32[16,64,128]{2,1,0:T(8,128)S(1)} %bitcast.4) | data formatting | bytes 1048576

commit v4 on v3

--- a/solution.py
+++ b/solution.py
@@ -237,7 +237,7 @@
     u_raw, kx_raw, ky_raw, nat, turned, gx, gy,
     coef_x, kept_x, tree_x, tkept_x, every_x, weights_x, chain_x, mine_x, out_x, got_x,
     coef_y, kept_y, tree_y, tkept_y, every_y, weights_y, chain_y, mine_y, out_y, got_y,
-    edge_x_in, edge_y_out, edge_y_in, ends,
+    edge_x_in, edge_y_out, edge_y_in, ends, ports,
     local_sem, xs, xr, ys, yr,
 ):
     nz, lx, ly = dims
@@ -248,9 +248,12 @@
     iy = lax.axis_index("gy")
     loads = []
     for i, (src, dst) in enumerate(((ky_hbm, ky_raw), (u_hbm, u_raw), (kx_hbm, kx_raw))):
-        cp = pltpu.make_async_copy(src, dst, local_sem.at[i])
-        cp.start()
-        loads.append(cp)
+        parts = [
+            pltpu.make_async_copy(src.at[:, :, t, :], dst.at[:, t], local_sem.at[i, t]) for t in range(SUB)
+        ]
+        for part in parts:
+            part.start()
+        loads.append(parts)
     line_x = Line("gx", nx, ix, xs, xr)
     line_y = Line("gy", ny, iy, ys, yr)
     barrier = pltpu.get_barrier_semaphore()
@@ -258,11 +261,23 @@
         for _, target, _ in line.others():
             pl.semaphore_signal(barrier, inc=1, device_id={line.axis: target}, device_id_type=MESH)
 
+    planes = lanes // lx
+
+    def arrived(parts):
+        for part in parts:
+            part.wait()
+
     def group(ref, g):
-        return ref[g * lanes : (g + 1) * lanes]
-
-    def x_rows(ref, x):
-        return ref[pl.ds(x, nz, stride=lx), :]
+        return ref[g * planes : (g + 1) * planes].reshape(lanes, ly)
+
+    def by_block(v):
+        ports[...] = v.reshape(nz * bx, ly)
+        return jnp.stack([ports[pl.ds(b, nz, stride=bx), :] for b in range(bx)], axis=0)
+
+    def by_plane(v):
+        for b in range(bx):
+            ports[pl.ds(b, nz, stride=bx), :] = v[b]
+        return ports[...].reshape(nz, bx, ly)
 
     def y_rows(y):
         return turned[pl.ds(y, groups, stride=ly), :]
@@ -271,7 +286,7 @@
     hy = 2 * (ny - 1)
 
     def edge_x():
-        return line_x.copy(kx_hbm.reshape(nz, lx, ly).at[:, lx - 1, :], edge_x_in, hx, jnp.minimum(ix + 1, nx - 1))
+        return line_x.copy(kx_hbm.at[:, bx - 1, SUB - 1, :], edge_x_in.at[:, 0, :], hx, jnp.minimum(ix + 1, nx - 1))
 
     def edge_y_right():
         return line_y.copy(edge_y_out.at[1], edge_y_in.at[0], hy, jnp.minimum(iy + 1, ny - 1))
@@ -288,7 +303,7 @@
     lane = lax.broadcasted_iota(jnp.int32, (lanes, ly), 1)
     packed = None
     for kind, (load, raw) in enumerate(((loads[0], ky_raw), (loads[1], u_raw))):
-        load.wait()
+        arrived(load)
         for g in range(groups):
             at = 2 * (kind * groups + g)
             moved = pltpu.roll(group(raw, g), at + 1, 1)
@@ -306,20 +321,29 @@
     def _():
         edge_y_left().start()
 
-    loads[2].wait()
-    kx_first = x_rows(kx_raw, 0)
-    kx_last = x_rows(kx_raw, lx - 1)
-    prior = kx_first
-    for x in range(1, lx):
-        now = x_rows(kx_raw, x)
-        gx[x // SUB, x % SUB] = 0.5 * (prior + now)
+    for g in range(groups):
+        turned[g * ly : (g + 1) * ly] = group(ky_raw, g).T
+    prior = y_rows(0)
+    for y in range(1, ly):
+        now = y_rows(y)
+        gy[y // SUB, y % SUB] = 0.5 * (prior + now)
         prior = now
+    ky_last = prior
+
+    arrived(loads[2])
+    for t in range(1, SUB):
+        gx[:, t] = 0.5 * (kx_raw[:, t - 1] + kx_raw[:, t])
+    kx_ends = kx_raw[:, SUB - 1]
+    kx_last = by_block(kx_ends)[bx - 1]
+
     @pl.when(ix > 0)
     def _():
         edge_x().wait_recv()
 
-    gx[0, 0] = 0.5 * (jnp.where(ix > 0, edge_x_in[...], 0.0) + kx_first)
-    at_p, series, at_l = factor_tree(*factor_cells(lambda t: gx[:, t], coef_x), tree_x)
+    block = lax.broadcasted_iota(jnp.int32, (nz, bx, ly), 1)
+    prior = jnp.where(block > 0, pltpu.roll(kx_ends, 1, 1), jnp.where(ix > 0, edge_x_in[...], 0.0))
+    gx[:, 0] = 0.5 * (prior + kx_raw[:, 0])
+    at_p, series, at_l = factor_tree(*[by_block(v) for v in factor_cells(lambda t: gx[:, t], coef_x)], tree_x)
     at_l = at_l + jnp.where(ix == nx - 1, 0.5 * kx_last, 0.0)
     share_coefs(line_x, (at_p, series, at_l), every_x)
 
@@ -348,26 +372,15 @@
         flux = 0.5 * (k + pltpu.roll(k, 1, 1)) * (u - pltpu.roll(u, 1, 1))
         flux = jnp.where(lane > 0, flux, outer)
         later = jnp.where(lane < ly - 1, pltpu.roll(flux, ly - 1, 1), outer)
-        nat[g * lanes : (g + 1) * lanes] = u + (later - flux)
+        nat[g * planes : (g + 1) * planes] = (u + (later - flux)).reshape(planes, SUB, bx, ly)
 
     await_coefs(line_x, every_x)
-    def x_cells(t):
-        return jnp.stack([x_rows(nat, b * SUB + t) for b in range(bx)], axis=0)
-
-    d_p, d_l = down_cells(x_cells, coef_x, kept_x)
-    d_p, d_l = down_tree(d_p, d_l, tree_x, tkept_x)
+    d_p, d_l = down_cells(lambda t: nat[:, t], coef_x, kept_x)
+    d_p, d_l = down_tree(by_block(d_p), by_block(d_l), tree_x, tkept_x)
     line_ratios(ix, nx, every_x, chain_x, mine_x)
     send_values(line_x, d_p, d_l, out_x, got_x, mine_x)
 
     inverses = line_weights(ix, nx, chain_x, mine_x, weights_x)
-    for g in range(groups):
-        turned[g * ly : (g + 1) * ly] = group(ky_raw, g).T
-    prior = y_rows(0)
-    for y in range(1, ly):
-        now = y_rows(y)
-        gy[y // SUB, y % SUB] = 0.5 * (prior + now)
-        prior = now
-    ky_last = prior
     at_p, series, at_l = factor_tree(*factor_cells(lambda t: gy[:, t], coef_y), tree_y)
     at_l = at_l + jnp.where(iy == ny - 1, 0.5 * ky_last, 0.0)
     share_coefs(line_y, (at_p, series, at_l), every_y)
@@ -376,10 +389,9 @@
     before, nodes = up_tree(u_p, u_l, tree_x, tkept_x)
 
     def put_x(t, v):
-        for b in range(bx):
-            nat[pl.ds(b * SUB + t, nz, stride=lx), :] = v[b]
-
-    up_cells(before, nodes, coef_x, kept_x, put_x)
+        nat[:, t] = v
+
+    up_cells(by_plane(before), by_plane(nodes), coef_x, kept_x, put_x)
     for g in range(groups):
         turned[g * ly : (g + 1) * ly] = (group(nat, g) - group(u_raw, g)).T
 
@@ -417,7 +429,11 @@
 
     up_cells(before, nodes, coef_y, kept_y, put_y)
     for g in range(groups):
-        out_ref[g * lanes : (g + 1) * lanes] = group(u_raw, g) + 2.0 * turned[g * ly : (g + 1) * ly].T
+        o = group(u_raw, g) + 2.0 * turned[g * ly : (g + 1) * ly].T
+        for p in range(planes):
+            for t in range(SUB):
+                at = p * lx + t * bx
+                out_ref[pl.ds(g * lanes + p * lx + t, bx, stride=SUB), :] = o[at : at + bx]
 
     line_y.done_sending(lambda o: out_y.at[0], got_y, ny - 1)
 
@@ -428,11 +444,11 @@
     flat = (nz * lx, ly)
     bx, by = lx // SUB, ly // SUB
 
-    def line_scratch(n, blocks, rows):
+    def line_scratch(n, blocks, rows, cells):
         one = (rows, 128)
         return [
-            pltpu.VMEM((3, SUB - 1, blocks) + one, F32),
-            pltpu.VMEM((SUB - 1, blocks) + one, F32),
+            pltpu.VMEM((3, SUB - 1) + cells, F32),
+            pltpu.VMEM((SUB - 1,) + cells, F32),
             pltpu.VMEM((3, blocks - 1) + one, F32),
             pltpu.VMEM((blocks - 1,) + one, F32),
             pltpu.VMEM((n, 3) + one, F32),
@@ -444,19 +460,21 @@
         ]
 
     scratch = (
-        [pltpu.VMEM(flat, F32)] * 5
+        [pltpu.VMEM((nz, SUB, bx, ly), F32)] * 4
         + [
-            pltpu.VMEM((bx, SUB, nz, ly), F32),
+            pltpu.VMEM(flat, F32),
+            pltpu.VMEM((nz, SUB, bx, ly), F32),
             pltpu.VMEM((by, SUB, groups, 128), F32),
         ]
-        + line_scratch(nx, bx, nz)
-        + line_scratch(ny, by, groups)
+        + line_scratch(nx, bx, nz, (nz, bx, ly))
+        + line_scratch(ny, by, groups, (by, groups, 128))
         + [
-            pltpu.VMEM((nz, ly), F32),
+            pltpu.VMEM((nz, bx, ly), F32),
             pltpu.VMEM((2, 2, groups, 128), F32),
             pltpu.VMEM((2, 2, groups, 128), F32),
             pltpu.VMEM((128, 128), F32),
-            pltpu.SemaphoreType.DMA((3,)),
+            pltpu.VMEM((nz * bx, ly), F32),
+            pltpu.SemaphoreType.DMA((3, SUB)),
             pltpu.SemaphoreType.DMA((2 * nx - 1,)),
             pltpu.SemaphoreType.DMA((2 * nx - 1,)),
             pltpu.SemaphoreType.DMA((2 * ny,)),
@@ -472,7 +490,7 @@
         compiler_params=pltpu.CompilerParams(
             collective_id=0, has_side_effects=True, vmem_limit_bytes=32 * 1024 * 1024
         ),
-    )(*[pltpu.with_memory_space_constraint(v.reshape(flat), pltpu.HBM) for v in (state, kappa_x, kappa_y)])
+    )(*[pltpu.with_memory_space_constraint(v.reshape(nz, bx, SUB, ly), pltpu.HBM) for v in (state, kappa_x, kappa_y)])
     return out.reshape(state.shape)
 
 

time: 23.3 us -> 22.8 us (0.979)
  Pallas kernels: 22.3 us -> 21.9 us
    pallas_call x1, Pallas kernels: 22.3 us -> 21.9 us  [on_device(): pl.pallas_call(functools.partial(kernel, nx, ny, (nz, lx, ly)), out_shape...]
where the time goes in v4:
time: 22.8 us; the launch traced here: 22.7 us
  Pallas kernels  21.9 us (96%)
  local copies, waits for them, and re-layouts  0.8 us (4%)
    pallas_call x1, Pallas kernels, on_device(): pl.pallas_call(functools.partial(kernel, nx, ny, (nz, lx, ly)), out_shape...  21.9 us
    unnamed x1, local copies, waits for them, and re-layouts  0.8 us

profile of v4, /device:TPU:0, one launch (start us, length us, event | category | flops | bytes accessed | tf_op | source)
XLA Modules:
  0.0 22.7 jit_solution(1579997558109682985)
XLA Ops:
  0.0 21.9 %shard_map.37 = f32[1024,128]{1,0:T(8,128)S(1)} custom-call(f32[16,8,8,128]{3,2,1,0:T(8,128)} %bitcast.5, f32[16,8,8,128]{3,2,1,0:T(8,128)} %bitcast.6, f32[16,8,8,128]{3,2,1,0:T(8,128)} %bitcast.7), custom_call_target="tpu_custom_call" | custom-call | tf_op jit(solution)/shard_map/pallas_call | solution.py:484
  21.9 0.8 %copy.5 = f32[16,64,128]{2,1,0:T(8,128)} copy(f32[16,64,128]{2,1,0:T(8,128)S(1)} %bitcast.4) | data formatting | bytes 1048576

commit v5 on v4

--- a/solution.py
+++ b/solution.py
@@ -17,22 +17,28 @@
     return r * (2.0 - p * r)
 
 
-def factor_cells(face, coef):
-    s = jnp.ones_like(face(0))
+def loop(count, body):
+    lax.fori_loop(0, count, lambda i, c: (body(i), c)[1], 0)
+
+
+def factor_cells(face, coef, chunk, ports):
     to_p = face(0)
+    s = jnp.ones_like(to_p)
     at_p = jnp.zeros_like(s)
     for t in range(SUB - 1):
         right = face(t + 1)
         r = recip(s + to_p + right)
         a = right * r
         b = to_p * r
-        coef[0, t] = r
-        coef[1, t] = a
-        coef[2, t] = b
+        coef[0, t, chunk] = r
+        coef[1, t, chunk] = a
+        coef[2, t, chunk] = b
         at_p = at_p + s * b
         s = 1.0 + s * a
         to_p = to_p * a
-    return at_p, to_p, s
+    ports[0, chunk] = at_p
+    ports[1, chunk] = to_p
+    ports[2, chunk] = s
 
 
 def halves(v):
@@ -63,15 +69,16 @@
     return at_p[0], series[0], at_l[0]
 
 
-def down_cells(source, coef, kept):
+def down_cells(source, coef, kept, chunk, ports):
     d = source(0)
     at_p = None
     for t in range(SUB - 1):
-        kept[t] = d
-        share = coef[2, t] * d
+        kept[t, chunk] = d
+        share = coef[2, t, chunk] * d
         at_p = share if at_p is None else at_p + share
-        d = source(t + 1) + coef[1, t] * d
-    return at_p, d
+        d = source(t + 1) + coef[1, t, chunk] * d
+    ports[0, chunk] = at_p
+    ports[1, chunk] = d
 
 
 def down_tree(at_p, at_l, tree, kept):
@@ -107,11 +114,12 @@
     return before, nodes
 
 
-def up_cells(before, nodes, coef, kept, put):
-    u = nodes
+def up_cells(coef, kept, put, chunk, ports):
+    before = ports[0, chunk]
+    u = ports[1, chunk]
     put(SUB - 1, u)
     for t in range(SUB - 2, -1, -1):
-        u = coef[0, t] * kept[t] + coef[1, t] * u + coef[2, t] * before
+        u = coef[0, t, chunk] * kept[t, chunk] + coef[1, t, chunk] * u + coef[2, t, chunk] * before
         put(t, u)
 
 
@@ -234,10 +242,10 @@
 def kernel(
     nx, ny, dims,
     u_hbm, kx_hbm, ky_hbm, out_ref,
-    u_raw, kx_raw, ky_raw, nat, turned, gx, gy,
+    u_raw, kx_raw, ky_raw, nat, turned, k_before, ports_x, ports_y,
     coef_x, kept_x, tree_x, tkept_x, every_x, weights_x, chain_x, mine_x, out_x, got_x,
     coef_y, kept_y, tree_y, tkept_y, every_y, weights_y, chain_y, mine_y, out_y, got_y,
-    edge_x_in, edge_y_out, edge_y_in, ends, ports,
+    edge_x_in, edge_y_out, edge_y_in, ends,
     local_sem, xs, xr, ys, yr,
 ):
     nz, lx, ly = dims
@@ -268,16 +276,29 @@
             part.wait()
 
     def group(ref, g):
-        return ref[g * planes : (g + 1) * planes].reshape(lanes, ly)
-
-    def by_block(v):
-        ports[...] = v.reshape(nz * bx, ly)
-        return jnp.stack([ports[pl.ds(b, nz, stride=bx), :] for b in range(bx)], axis=0)
-
-    def by_plane(v):
+        return ref[pl.ds(g * planes, planes)].reshape(lanes, ly)
+
+    def by_block(i):
+        rows = ports_x.at[i].reshape(nz * bx, ly)
+        return jnp.stack([rows[pl.ds(b, nz, stride=bx), :] for b in range(bx)], axis=0)
+
+    def by_plane(i, v):
+        rows = ports_x.at[i].reshape(nz * bx, ly)
         for b in range(bx):
-            ports[pl.ds(b, nz, stride=bx), :] = v[b]
-        return ports[...].reshape(nz, bx, ly)
+            rows[pl.ds(b, nz, stride=bx), :] = v[b]
+
+    def chunks(total, parts):
+        size = total // parts
+        return lambda c: pl.ds(c * size, size)
+
+    x2, x4 = chunks(nz, 2), chunks(nz, 4)
+    y2, y4 = chunks(by, 2), chunks(by, 4)
+
+    def y_cells(c, parts, t):
+        size = by // parts
+        return jnp.stack(
+            [turned[pl.ds((c * size + b) * SUB + t, groups, stride=ly), :] for b in range(size)], axis=0
+        )
 
     def y_rows(y):
         return turned[pl.ds(y, groups, stride=ly), :]
@@ -301,14 +322,17 @@
         edge_x().start()
 
     lane = lax.broadcasted_iota(jnp.int32, (lanes, ly), 1)
-    packed = None
+    ends[...] = jnp.zeros_like(ends)
     for kind, (load, raw) in enumerate(((loads[0], ky_raw), (loads[1], u_raw))):
         arrived(load)
-        for g in range(groups):
+
+        def pack(g, packed):
             at = 2 * (kind * groups + g)
-            moved = pltpu.roll(group(raw, g), at + 1, 1)
-            packed = moved if packed is None else jnp.where(lane >= at, moved, packed)
-    ends[...] = packed.T
+            return jnp.where(lane >= at, pltpu.roll(group(raw, g), at + 1, 1), packed)
+
+        packed = lax.fori_loop(0, groups, pack, ends[...])
+        ends[...] = packed
+    ends[...] = ends[...].T
     for kind in range(2):
         for side in range(2):
             edge_y_out[side, kind] = ends[pl.ds(2 * kind * groups + 1 - side, groups, stride=2), :]
@@ -321,29 +345,30 @@
     def _():
         edge_y_left().start()
 
-    for g in range(groups):
-        turned[g * ly : (g + 1) * ly] = group(ky_raw, g).T
-    prior = y_rows(0)
-    for y in range(1, ly):
-        now = y_rows(y)
-        gy[y // SUB, y % SUB] = 0.5 * (prior + now)
-        prior = now
-    ky_last = prior
+    def turn_k(g):
+        turned[pl.ds(pl.multiple_of(g * ly, ly), ly), :] = group(ky_raw, g).T
+
+    loop(groups, turn_k)
+    ky_last = y_rows(ly - 1)
+    for b in range(1, by):
+        k_before[b] = y_rows(b * SUB - 1)
 
     arrived(loads[2])
-    for t in range(1, SUB):
-        gx[:, t] = 0.5 * (kx_raw[:, t - 1] + kx_raw[:, t])
-    kx_ends = kx_raw[:, SUB - 1]
-    kx_last = by_block(kx_ends)[bx - 1]
-
     @pl.when(ix > 0)
     def _():
         edge_x().wait_recv()
 
-    block = lax.broadcasted_iota(jnp.int32, (nz, bx, ly), 1)
-    prior = jnp.where(block > 0, pltpu.roll(kx_ends, 1, 1), jnp.where(ix > 0, edge_x_in[...], 0.0))
-    gx[:, 0] = 0.5 * (prior + kx_raw[:, 0])
-    at_p, series, at_l = factor_tree(*[by_block(v) for v in factor_cells(lambda t: gx[:, t], coef_x)], tree_x)
+    block = lax.broadcasted_iota(jnp.int32, (nz // 2, bx, ly), 1)
+
+    def factor_x(c):
+        k = [kx_raw[x2(c), t] for t in range(SUB)]
+        prior = jnp.where(block > 0, pltpu.roll(k[SUB - 1], 1, 1), jnp.where(ix > 0, edge_x_in[x2(c)], 0.0))
+        factor_cells(lambda t: 0.5 * ((k[t - 1] if t else prior) + k[t]), coef_x, x2(c), ports_x)
+        ports_x[3, x2(c)] = k[SUB - 1]
+
+    loop(2, factor_x)
+    at_p, series, at_l = factor_tree(by_block(0), by_block(1), by_block(2), tree_x)
+    kx_last = ports_x.at[3].reshape(nz * bx, ly)[pl.ds(bx - 1, nz, stride=bx), :]
     at_l = at_l + jnp.where(ix == nx - 1, 0.5 * kx_last, 0.0)
     share_coefs(line_x, (at_p, series, at_l), every_x)
 
@@ -358,49 +383,65 @@
     k0, u0, k1, u1 = edge_y_out[0, 0], edge_y_out[0, 1], edge_y_out[1, 0], edge_y_out[1, 1]
     inner, last = iy > 0, iy < ny - 1
     face_0 = 0.5 * (jnp.where(inner, edge_y_in[0, 0], 0.0) + k0)
-    gy[0, 0] = face_0
+    k_before[0] = jnp.where(inner, edge_y_in[0, 0], 0.0)
     face_1 = 0.5 * (jnp.where(last, edge_y_in[1, 0], 0.0) + k1)
     flux_0 = face_0 * (jnp.where(inner, edge_y_in[0, 1], 0.0) - u0)
     flux_1 = face_1 * (jnp.where(last, edge_y_in[1, 1], 0.0) - u1)
     ends[pl.ds(0, groups, stride=2), :] = flux_1
     ends[pl.ds(1, groups, stride=2), :] = -flux_0
     fluxes = ends[...].T
-    for g in range(groups):
-        outer = pltpu.roll(fluxes, (ly - 2 * g - 1) % ly, 1)
+
+    def sources(g):
+        outer = pltpu.roll(fluxes, ly - 2 * g - 1, 1)
         u = group(u_raw, g)
         k = group(ky_raw, g)
         flux = 0.5 * (k + pltpu.roll(k, 1, 1)) * (u - pltpu.roll(u, 1, 1))
         flux = jnp.where(lane > 0, flux, outer)
         later = jnp.where(lane < ly - 1, pltpu.roll(flux, ly - 1, 1), outer)
-        nat[g * planes : (g + 1) * planes] = (u + (later - flux)).reshape(planes, SUB, bx, ly)
-
+        nat[pl.ds(g * planes, planes)] = (u + (later - flux)).reshape(planes, SUB, bx, ly)
+
+    loop(groups, sources)
     await_coefs(line_x, every_x)
-    d_p, d_l = down_cells(lambda t: nat[:, t], coef_x, kept_x)
-    d_p, d_l = down_tree(by_block(d_p), by_block(d_l), tree_x, tkept_x)
+    loop(4, lambda c: down_cells(lambda t: nat[x4(c), t], coef_x, kept_x, x4(c), ports_x))
+    d_p, d_l = down_tree(by_block(0), by_block(1), tree_x, tkept_x)
     line_ratios(ix, nx, every_x, chain_x, mine_x)
     send_values(line_x, d_p, d_l, out_x, got_x, mine_x)
 
     inverses = line_weights(ix, nx, chain_x, mine_x, weights_x)
-    at_p, series, at_l = factor_tree(*factor_cells(lambda t: gy[:, t], coef_y), tree_y)
+
+    def factor_y(c):
+        def face(t):
+            prior = y_cells(c, 2, t - 1) if t else k_before[y2(c)]
+            return 0.5 * (prior + y_cells(c, 2, t))
+
+        factor_cells(face, coef_y, y2(c), ports_y)
+
+    loop(2, factor_y)
+    at_p, series, at_l = factor_tree(ports_y[0], ports_y[1], ports_y[2], tree_y)
     at_l = at_l + jnp.where(iy == ny - 1, 0.5 * ky_last, 0.0)
     share_coefs(line_y, (at_p, series, at_l), every_y)
 
     u_p, u_l = take_values(line_x, inverses, out_x, got_x, weights_x)
     before, nodes = up_tree(u_p, u_l, tree_x, tkept_x)
 
-    def put_x(t, v):
-        nat[:, t] = v
-
-    up_cells(by_plane(before), by_plane(nodes), coef_x, kept_x, put_x)
-    for g in range(groups):
-        turned[g * ly : (g + 1) * ly] = (group(nat, g) - group(u_raw, g)).T
-
-    def y_cells(t):
-        return jnp.stack([y_rows(b * SUB + t) for b in range(by)], axis=0)
-
+    by_plane(0, before)
+    by_plane(1, nodes)
+
+    def up_x(c):
+        def put(t, v):
+            nat[x4(c), t] = v
+
+        up_cells(coef_x, kept_x, put, x4(c), ports_x)
+
+    loop(4, up_x)
+
+    def turn_q(g):
+        turned[pl.ds(pl.multiple_of(g * ly, ly), ly), :] = (group(nat, g) - group(u_raw, g)).T
+
+    loop(groups, turn_q)
     await_coefs(line_y, every_y)
-    d_p, d_l = down_cells(y_cells, coef_y, kept_y)
-    d_p, d_l = down_tree(d_p, d_l, tree_y, tkept_y)
+    loop(4, lambda c: down_cells(lambda t: y_cells(c, 4, t), coef_y, kept_y, y4(c), ports_y))
+    d_p, d_l = down_tree(ports_y[0], ports_y[1], tree_y, tkept_y)
     line_ratios(iy, ny, every_y, chain_y, mine_y)
     send_values(line_y, d_p, d_l, out_y, got_y, mine_y)
     inverses = line_weights(iy, ny, chain_y, mine_y, weights_y)
@@ -423,18 +464,28 @@
     u_p, u_l = take_values(line_y, inverses, out_y, got_y, weights_y)
     before, nodes = up_tree(u_p, u_l, tree_y, tkept_y)
 
-    def put_y(t, v):
-        for b in range(by):
-            turned[pl.ds(b * SUB + t, groups, stride=ly), :] = v[b]
-
-    up_cells(before, nodes, coef_y, kept_y, put_y)
-    for g in range(groups):
-        o = group(u_raw, g) + 2.0 * turned[g * ly : (g + 1) * ly].T
+    ports_y[0] = before
+    ports_y[1] = nodes
+
+    def up_y(c):
+        def put(t, v):
+            size = by // 4
+            for b in range(size):
+                turned[pl.ds((c * size + b) * SUB + t, groups, stride=ly), :] = v[b]
+
+        up_cells(coef_y, kept_y, put, y4(c), ports_y)
+
+    loop(4, up_y)
+
+    def finish(g):
+        w = turned[pl.ds(pl.multiple_of(g * ly, ly), ly), :].T
+        o = group(u_raw, g) + 2.0 * w
         for p in range(planes):
             for t in range(SUB):
                 at = p * lx + t * bx
                 out_ref[pl.ds(g * lanes + p * lx + t, bx, stride=SUB), :] = o[at : at + bx]
 
+    loop(groups, finish)
     line_y.done_sending(lambda o: out_y.at[0], got_y, ny - 1)
 
 
@@ -463,8 +514,9 @@
         [pltpu.VMEM((nz, SUB, bx, ly), F32)] * 4
         + [
             pltpu.VMEM(flat, F32),
-            pltpu.VMEM((nz, SUB, bx, ly), F32),
-            pltpu.VMEM((by, SUB, groups, 128), F32),
+            pltpu.VMEM((by, groups, 128), F32),
+            pltpu.VMEM((4, nz, bx, ly), F32),
+            pltpu.VMEM((3, by, groups, 128), F32),
         ]
         + line_scratch(nx, bx, nz, (nz, bx, ly))
         + line_scratch(ny, by, groups, (by, groups, 128))
@@ -473,7 +525,6 @@
             pltpu.VMEM((2, 2, groups, 128), F32),
             pltpu.VMEM((2, 2, groups, 128), F32),
             pltpu.VMEM((128, 128), F32),
-            pltpu.VMEM((nz * bx, ly), F32),
             pltpu.SemaphoreType.DMA((3, SUB)),
             pltpu.SemaphoreType.DMA((2 * nx - 1,)),
             pltpu.SemaphoreType.DMA((2 * nx - 1,)),

time: 22.8 us -> 24.9 us (1.092)
  Pallas kernels: 21.9 us -> 24 us
    pallas_call x1, Pallas kernels: 21.9 us -> 24 us  [on_device(): pl.pallas_call(functools.partial(kernel, nx, ny, (nz, lx, ly)), out_shape...]
where the time goes in v5:
time: 24.9 us; the launch traced here: 24.8 us
  Pallas kernels  24 us (96%)
  local copies, waits for them, and re-layouts  0.8 us (3%)
    pallas_call x1, Pallas kernels, on_device(): pl.pallas_call(functools.partial(kernel, nx, ny, (nz, lx, ly)), out_shape...  24 us
    unnamed x1, local copies, waits for them, and re-layouts  0.8 us

profile of v5, /device:TPU:0, one launch (start us, length us, event | category | flops | bytes accessed | tf_op | source)
XLA Modules:
  0.0 24.8 jit_solution(5250392090657790558)
XLA Ops:
  0.0 24.0 %shard_map.37 = f32[1024,128]{1,0:T(8,128)S(1)} custom-call(f32[16,8,8,128]{3,2,1,0:T(8,128)} %bitcast.5, f32[16,8,8,128]{3,2,1,0:T(8,128)} %bitcast.6, f32[16,8,8,128]{3,2,1,0:T(8,128)} %bitcast.7), custom_call_target="tpu_custom_call" | custom-call | tf_op jit(solution)/shard_map/pallas_call | solution.py:535
  24.0 0.8 %copy.5 = f32[16,64,128]{2,1,0:T(8,128)} copy(f32[16,64,128]{2,1,0:T(8,128)S(1)} %bitcast.4) | data formatting | bytes 1048576

commit v6 on v3

--- a/solution.py
+++ b/solution.py
@@ -306,6 +306,15 @@
     def _():
         edge_y_left().start()
 
+    for g in range(groups):
+        turned[g * ly : (g + 1) * ly] = group(ky_raw, g).T
+    prior = y_rows(0)
+    for y in range(1, ly):
+        now = y_rows(y)
+        gy[y // SUB, y % SUB] = 0.5 * (prior + now)
+        prior = now
+    ky_last = prior
+
     loads[2].wait()
     kx_first = x_rows(kx_raw, 0)
     kx_last = x_rows(kx_raw, lx - 1)
@@ -314,6 +323,7 @@
         now = x_rows(kx_raw, x)
         gx[x // SUB, x % SUB] = 0.5 * (prior + now)
         prior = now
+
     @pl.when(ix > 0)
     def _():
         edge_x().wait_recv()
@@ -350,24 +360,16 @@
         later = jnp.where(lane < ly - 1, pltpu.roll(flux, ly - 1, 1), outer)
         nat[g * lanes : (g + 1) * lanes] = u + (later - flux)
 
-    await_coefs(line_x, every_x)
     def x_cells(t):
         return jnp.stack([x_rows(nat, b * SUB + t) for b in range(bx)], axis=0)
 
     d_p, d_l = down_cells(x_cells, coef_x, kept_x)
     d_p, d_l = down_tree(d_p, d_l, tree_x, tkept_x)
+    await_coefs(line_x, every_x)
     line_ratios(ix, nx, every_x, chain_x, mine_x)
     send_values(line_x, d_p, d_l, out_x, got_x, mine_x)
 
     inverses = line_weights(ix, nx, chain_x, mine_x, weights_x)
-    for g in range(groups):
-        turned[g * ly : (g + 1) * ly] = group(ky_raw, g).T
-    prior = y_rows(0)
-    for y in range(1, ly):
-        now = y_rows(y)
-        gy[y // SUB, y % SUB] = 0.5 * (prior + now)
-        prior = now
-    ky_last = prior
     at_p, series, at_l = factor_tree(*factor_cells(lambda t: gy[:, t], coef_y), tree_y)
     at_l = at_l + jnp.where(iy == ny - 1, 0.5 * ky_last, 0.0)
     share_coefs(line_y, (at_p, series, at_l), every_y)

time: 23.3 us -> 22.6 us (0.970)
  Pallas kernels: 22.3 us -> 21.6 us
    pallas_call x1, Pallas kernels: 22.3 us -> 21.6 us  [on_device(): pl.pallas_call(functools.partial(kernel, nx, ny, (nz, lx, ly)), out_shape...]
where the time goes in v6:
time: 22.6 us; the launch traced here: 22.4 us
  Pallas kernels  21.6 us (96%)
  local copies, waits for them, and re-layouts  0.8 us (4%)
    pallas_call x1, Pallas kernels, on_device(): pl.pallas_call(functools.partial(kernel, nx, ny, (nz, lx, ly)), out_shape...  21.6 us
    unnamed x1, local copies, waits for them, and re-layouts  0.8 us

profile of v6, /device:TPU:0, one launch (start us, length us, event | category | flops | bytes accessed | tf_op | source)
XLA Modules:
  0.0 22.4 jit_solution(9056115930409213780)
XLA Ops:
  0.0 21.6 %shard_map.37 = f32[1024,128]{1,0:T(8,128)S(1)} custom-call(f32[1024,128]{1,0:T(8,128)} %bitcast.5, f32[1024,128]{1,0:T(8,128)} %bitcast.6, f32[1024,128]{1,0:T(8,128)} %bitcast.7), custom_call_target="tpu_custom_call" | custom-call | tf_op jit(solution)/shard_map/pallas_call | solution.py:468
  21.6 0.8 %copy.5 = f32[16,64,128]{2,1,0:T(8,128)} copy(f32[16,64,128]{2,1,0:T(8,128)S(1)} %bitcast.4) | data formatting | bytes 1048576

commit v7 on v6

--- a/solution.py
+++ b/solution.py
@@ -306,6 +306,24 @@
     def _():
         edge_y_left().start()
 
+    loads[2].wait()
+    kx_first = x_rows(kx_raw, 0)
+    kx_last = x_rows(kx_raw, lx - 1)
+    prior = kx_first
+    for x in range(1, lx):
+        now = x_rows(kx_raw, x)
+        gx[x // SUB, x % SUB] = 0.5 * (prior + now)
+        prior = now
+
+    @pl.when(ix > 0)
+    def _():
+        edge_x().wait_recv()
+
+    gx[0, 0] = 0.5 * (jnp.where(ix > 0, edge_x_in[...], 0.0) + kx_first)
+    at_p, series, at_l = factor_tree(*factor_cells(lambda t: gx[:, t], coef_x), tree_x)
+    at_l = at_l + jnp.where(ix == nx - 1, 0.5 * kx_last, 0.0)
+    share_coefs(line_x, (at_p, series, at_l), every_x)
+
     for g in range(groups):
         turned[g * ly : (g + 1) * ly] = group(ky_raw, g).T
     prior = y_rows(0)
@@ -315,24 +333,6 @@
         prior = now
     ky_last = prior
 
-    loads[2].wait()
-    kx_first = x_rows(kx_raw, 0)
-    kx_last = x_rows(kx_raw, lx - 1)
-    prior = kx_first
-    for x in range(1, lx):
-        now = x_rows(kx_raw, x)
-        gx[x // SUB, x % SUB] = 0.5 * (prior + now)
-        prior = now
-
-    @pl.when(ix > 0)
-    def _():
-        edge_x().wait_recv()
-
-    gx[0, 0] = 0.5 * (jnp.where(ix > 0, edge_x_in[...], 0.0) + kx_first)
-    at_p, series, at_l = factor_tree(*factor_cells(lambda t: gx[:, t], coef_x), tree_x)
-    at_l = at_l + jnp.where(ix == nx - 1, 0.5 * kx_last, 0.0)
-    share_coefs(line_x, (at_p, series, at_l), every_x)
-
     @pl.when(iy > 0)
     def _():
         edge_y_right().wait_recv()
@@ -348,6 +348,11 @@
     face_1 = 0.5 * (jnp.where(last, edge_y_in[1, 0], 0.0) + k1)
     flux_0 = face_0 * (jnp.where(inner, edge_y_in[0, 1], 0.0) - u0)
     flux_1 = face_1 * (jnp.where(last, edge_y_in[1, 1], 0.0) - u1)
+    at_p, series, at_l = factor_tree(*factor_cells(lambda t: gy[:, t], coef_y), tree_y)
+    at_l = at_l + jnp.where(iy == ny - 1, 0.5 * ky_last, 0.0)
+    share_coefs(line_y, (at_p, series, at_l), every_y)
+
+
     ends[pl.ds(0, groups, stride=2), :] = flux_1
     ends[pl.ds(1, groups, stride=2), :] = -flux_0
     fluxes = ends[...].T
@@ -370,10 +375,9 @@
     send_values(line_x, d_p, d_l, out_x, got_x, mine_x)
 
     inverses = line_weights(ix, nx, chain_x, mine_x, weights_x)
-    at_p, series, at_l = factor_tree(*factor_cells(lambda t: gy[:, t], coef_y), tree_y)
-    at_l = at_l + jnp.where(iy == ny - 1, 0.5 * ky_last, 0.0)
-    share_coefs(line_y, (at_p, series, at_l), every_y)
-
+    await_coefs(line_y, every_y)
+    line_ratios(iy, ny, every_y, chain_y, mine_y)
+    inverses_y = line_weights(iy, ny, chain_y, mine_y, weights_y)
     u_p, u_l = take_values(line_x, inverses, out_x, got_x, weights_x)
     before, nodes = up_tree(u_p, u_l, tree_x, tkept_x)
 
@@ -388,12 +392,9 @@
     def y_cells(t):
         return jnp.stack([y_rows(b * SUB + t) for b in range(by)], axis=0)
 
-    await_coefs(line_y, every_y)
     d_p, d_l = down_cells(y_cells, coef_y, kept_y)
     d_p, d_l = down_tree(d_p, d_l, tree_y, tkept_y)
-    line_ratios(iy, ny, every_y, chain_y, mine_y)
     send_values(line_y, d_p, d_l, out_y, got_y, mine_y)
-    inverses = line_weights(iy, ny, chain_y, mine_y, weights_y)
     line_x.done_sending(lambda o: every_x.at[ix], every_x, 0)
     line_x.done_sending(lambda o: out_x.at[0], got_x, nx - 1)
     line_y.done_sending(lambda o: every_y.at[iy], every_y, 0)
@@ -410,7 +411,7 @@
     def _():
         edge_y_left().wait_send()
 
-    u_p, u_l = take_values(line_y, inverses, out_y, got_y, weights_y)
+    u_p, u_l = take_values(line_y, inverses_y, out_y, got_y, weights_y)
     before, nodes = up_tree(u_p, u_l, tree_y, tkept_y)
 
     def put_y(t, v):

time: 22.6 us -> 20.8 us (0.920)
  Pallas kernels: 21.6 us -> 19.9 us
    pallas_call x1, Pallas kernels: 21.6 us -> 19.9 us  [on_device(): pl.pallas_call(functools.partial(kernel, nx, ny, (nz, lx, ly)), out_shape...]
where the time goes in v7:
time: 20.8 us; the launch traced here: 20.7 us
  Pallas kernels  19.9 us (96%)
  local copies, waits for them, and re-layouts  0.8 us (4%)
    pallas_call x1, Pallas kernels, on_device(): pl.pallas_call(functools.partial(kernel, nx, ny, (nz, lx, ly)), out_shape...  19.9 us
    unnamed x1, local copies, waits for them, and re-layouts  0.8 us

profile of v7, /device:TPU:0, one launch (start us, length us, event | category | flops | bytes accessed | tf_op | source)
XLA Modules:
  0.0 20.7 jit_solution(1099927972497020669)
XLA Ops:
  0.0 19.9 %shard_map.37 = f32[1024,128]{1,0:T(8,128)S(1)} custom-call(f32[1024,128]{1,0:T(8,128)} %bitcast.5, f32[1024,128]{1,0:T(8,128)} %bitcast.6, f32[1024,128]{1,0:T(8,128)} %bitcast.7), custom_call_target="tpu_custom_call" | custom-call | tf_op jit(solution)/shard_map/pallas_call | solution.py:469
  19.9 0.8 %copy.5 = f32[16,64,128]{2,1,0:T(8,128)} copy(f32[16,64,128]{2,1,0:T(8,128)S(1)} %bitcast.4) | data formatting | bytes 1048576

commit v8 on v7

--- a/solution.py
+++ b/solution.py
@@ -10,6 +10,7 @@
 MESH = pl.DeviceIdType.MESH
 F32 = jnp.float32
 SUB = 8
+PARTS = 4
 
 
 def recip(p):
@@ -17,22 +18,33 @@
     return r * (2.0 - p * r)
 
 
-def factor_cells(face, coef):
-    s = jnp.ones_like(face(0))
-    to_p = face(0)
-    at_p = jnp.zeros_like(s)
-    for t in range(SUB - 1):
-        right = face(t + 1)
-        r = recip(s + to_p + right)
-        a = right * r
-        b = to_p * r
-        coef[0, t] = r
-        coef[1, t] = a
-        coef[2, t] = b
-        at_p = at_p + s * b
-        s = 1.0 + s * a
-        to_p = to_p * a
-    return at_p, to_p, s
+def factor_cells(row, before_first, coef, blocks):
+    ports = []
+    for part in range(2):
+        half = range(part * blocks // 2, (part + 1) * blocks // 2)
+
+        def cells(t):
+            return jnp.stack([row(b * SUB + t) if b * SUB + t >= 0 else before_first for b in half], axis=0)
+
+        now = cells(0)
+        to_p = 0.5 * (cells(-1) + now)
+        s = jnp.ones_like(to_p)
+        at_p = jnp.zeros_like(s)
+        for t in range(SUB - 1):
+            later = cells(t + 1)
+            right = 0.5 * (now + later)
+            now = later
+            r = recip(s + to_p + right)
+            a = right * r
+            b = to_p * r
+            coef[0, t, half.start : half.stop] = r
+            coef[1, t, half.start : half.stop] = a
+            coef[2, t, half.start : half.stop] = b
+            at_p = at_p + s * b
+            s = 1.0 + s * a
+            to_p = to_p * a
+        ports.append((at_p, to_p, s))
+    return [jnp.concatenate(both, axis=0) for both in zip(*ports)]
 
 
 def halves(v):
@@ -186,7 +198,7 @@
         )
 
     def others(self):
-        for o in range(1, self.n):
+        for o in sorted(range(1, self.n), key=lambda o: abs(2 * o - self.n)):
             yield o, lax.rem(self.me + o, self.n), lax.rem(self.me + self.n - o, self.n)
 
     def start_all(self, src_of, buf, base):
@@ -223,7 +235,7 @@
 def take_values(line, inverses, out, got, weights):
     u_p = inverses[0] * out[1]
     u_l = inverses[1] * out[0]
-    for o, _, source in line.others():
+    for o, _, source in reversed(list(line.others())):
         line.await_one(o, out.at[0], got, line.n - 1)
         v = got[source]
         u_p = u_p + weights[source, 0] * v
@@ -234,7 +246,7 @@
 def kernel(
     nx, ny, dims,
     u_hbm, kx_hbm, ky_hbm, out_ref,
-    u_raw, kx_raw, ky_raw, nat, turned, gx, gy,
+    u_raw, kx_raw, ky_raw, nat, turned,
     coef_x, kept_x, tree_x, tkept_x, every_x, weights_x, chain_x, mine_x, out_x, got_x,
     coef_y, kept_y, tree_y, tkept_y, every_y, weights_y, chain_y, mine_y, out_y, got_y,
     edge_x_in, edge_y_out, edge_y_in, ends,
@@ -248,9 +260,14 @@
     iy = lax.axis_index("gy")
     loads = []
     for i, (src, dst) in enumerate(((ky_hbm, ky_raw), (u_hbm, u_raw), (kx_hbm, kx_raw))):
-        cp = pltpu.make_async_copy(src, dst, local_sem.at[i])
-        cp.start()
-        loads.append(cp)
+        size = nz * lx // PARTS
+        parts = [
+            pltpu.make_async_copy(src.at[pl.ds(p * size, size)], dst.at[pl.ds(p * size, size)], local_sem.at[i, p])
+            for p in range(PARTS)
+        ]
+        for part in parts:
+            part.start()
+        loads.append(parts)
     line_x = Line("gx", nx, ix, xs, xr)
     line_y = Line("gy", ny, iy, ys, yr)
     barrier = pltpu.get_barrier_semaphore()
@@ -288,7 +305,8 @@
     lane = lax.broadcasted_iota(jnp.int32, (lanes, ly), 1)
     packed = None
     for kind, (load, raw) in enumerate(((loads[0], ky_raw), (loads[1], u_raw))):
-        load.wait()
+        for part in load:
+            part.wait()
         for g in range(groups):
             at = 2 * (kind * groups + g)
             moved = pltpu.roll(group(raw, g), at + 1, 1)
@@ -306,32 +324,21 @@
     def _():
         edge_y_left().start()
 
-    loads[2].wait()
-    kx_first = x_rows(kx_raw, 0)
+    for part in loads[2]:
+        part.wait()
     kx_last = x_rows(kx_raw, lx - 1)
-    prior = kx_first
-    for x in range(1, lx):
-        now = x_rows(kx_raw, x)
-        gx[x // SUB, x % SUB] = 0.5 * (prior + now)
-        prior = now
-
     @pl.when(ix > 0)
     def _():
         edge_x().wait_recv()
 
-    gx[0, 0] = 0.5 * (jnp.where(ix > 0, edge_x_in[...], 0.0) + kx_first)
-    at_p, series, at_l = factor_tree(*factor_cells(lambda t: gx[:, t], coef_x), tree_x)
+    before_x = jnp.where(ix > 0, edge_x_in[...], 0.0)
+    at_p, series, at_l = factor_tree(*factor_cells(lambda x: x_rows(kx_raw, x), before_x, coef_x, bx), tree_x)
     at_l = at_l + jnp.where(ix == nx - 1, 0.5 * kx_last, 0.0)
     share_coefs(line_x, (at_p, series, at_l), every_x)
 
     for g in range(groups):
         turned[g * ly : (g + 1) * ly] = group(ky_raw, g).T
-    prior = y_rows(0)
-    for y in range(1, ly):
-        now = y_rows(y)
-        gy[y // SUB, y % SUB] = 0.5 * (prior + now)
-        prior = now
-    ky_last = prior
+    ky_last = y_rows(ly - 1)
 
     @pl.when(iy > 0)
     def _():
@@ -343,12 +350,12 @@
 
     k0, u0, k1, u1 = edge_y_out[0, 0], edge_y_out[0, 1], edge_y_out[1, 0], edge_y_out[1, 1]
     inner, last = iy > 0, iy < ny - 1
-    face_0 = 0.5 * (jnp.where(inner, edge_y_in[0, 0], 0.0) + k0)
-    gy[0, 0] = face_0
+    before_y = jnp.where(inner, edge_y_in[0, 0], 0.0)
+    face_0 = 0.5 * (before_y + k0)
     face_1 = 0.5 * (jnp.where(last, edge_y_in[1, 0], 0.0) + k1)
     flux_0 = face_0 * (jnp.where(inner, edge_y_in[0, 1], 0.0) - u0)
     flux_1 = face_1 * (jnp.where(last, edge_y_in[1, 1], 0.0) - u1)
-    at_p, series, at_l = factor_tree(*factor_cells(lambda t: gy[:, t], coef_y), tree_y)
+    at_p, series, at_l = factor_tree(*factor_cells(y_rows, before_y, coef_y, by), tree_y)
     at_l = at_l + jnp.where(iy == ny - 1, 0.5 * ky_last, 0.0)
     share_coefs(line_y, (at_p, series, at_l), every_y)
 
@@ -448,10 +455,6 @@
 
     scratch = (
         [pltpu.VMEM(flat, F32)] * 5
-        + [
-            pltpu.VMEM((bx, SUB, nz, ly), F32),
-            pltpu.VMEM((by, SUB, groups, 128), F32),
-        ]
         + line_scratch(nx, bx, nz)
         + line_scratch(ny, by, groups)
         + [
@@ -459,7 +462,7 @@
             pltpu.VMEM((2, 2, groups, 128), F32),
             pltpu.VMEM((2, 2, groups, 128), F32),
             pltpu.VMEM((128, 128), F32),
-            pltpu.SemaphoreType.DMA((3,)),
+            pltpu.SemaphoreType.DMA((3, PARTS)),
             pltpu.SemaphoreType.DMA((2 * nx - 1,)),
             pltpu.SemaphoreType.DMA((2 * nx - 1,)),
             pltpu.SemaphoreType.DMA((2 * ny,)),

time: 20.8 us -> 21.3 us (1.024)
  Pallas kernels: 19.9 us -> 20.4 us
    pallas_call x1, Pallas kernels: 19.9 us -> 20.4 us  [on_device(): pl.pallas_call(functools.partial(kernel, nx, ny, (nz, lx, ly)), out_shape...]
where the time goes in v8:
time: 21.3 us; the launch traced here: 21.2 us
  Pallas kernels  20.4 us (96%)
  local copies, waits for them, and re-layouts  0.8 us (4%)
    pallas_call x1, Pallas kernels, on_device(): pl.pallas_call(functools.partial(kernel, nx, ny, (nz, lx, ly)), out_shape...  20.4 us
    unnamed x1, local copies, waits for them, and re-layouts  0.8 us

profile of v8, /device:TPU:0, one launch (start us, length us, event | category | flops | bytes accessed | tf_op | source)
XLA Modules:
  0.0 21.2 jit_solution(1108589318011593984)
XLA Ops:
  0.0 20.4 %shard_map.37 = f32[1024,128]{1,0:T(8,128)S(1)} custom-call(f32[1024,128]{1,0:T(8,128)} %bitcast.5, f32[1024,128]{1,0:T(8,128)} %bitcast.6, f32[1024,128]{1,0:T(8,128)} %bitcast.7), custom_call_target="tpu_custom_call" | custom-call | tf_op jit(solution)/shard_map/pallas_call | solution.py:472
  20.4 0.8 %copy.5 = f32[16,64,128]{2,1,0:T(8,128)} copy(f32[16,64,128]{2,1,0:T(8,128)S(1)} %bitcast.4) | data formatting | bytes 1048576

commit v9 on v2

--- a/solution.py
+++ b/solution.py
@@ -314,6 +314,15 @@
         now = x_rows(kx_raw, x)
         gx[x // SUB, x % SUB] = 0.5 * (prior + now)
         prior = now
+    @pl.when(ix > 0)
+    def _():
+        edge_x().wait_recv()
+
+    gx[0, 0] = 0.5 * (jnp.where(ix > 0, edge_x_in[...], 0.0) + kx_first)
+    at_p, series, at_l = factor_tree(*factor_cells(lambda t: gx[:, t], coef_x), tree_x)
+    at_l = at_l + jnp.where(ix == nx - 1, 0.5 * kx_last, 0.0)
+    share_coefs(line_x, (at_p, series, at_l), every_x)
+
     for g in range(groups):
         turned[g * ly : (g + 1) * ly] = group(ky_raw, g).T
     prior = y_rows(0)
@@ -323,15 +332,6 @@
         prior = now
     ky_last = prior
 
-    @pl.when(ix > 0)
-    def _():
-        edge_x().wait_recv()
-
-    gx[0, 0] = 0.5 * (jnp.where(ix > 0, edge_x_in[...], 0.0) + kx_first)
-    at_p, series, at_l = factor_tree(*factor_cells(lambda t: gx[:, t], coef_x), tree_x)
-    at_l = at_l + jnp.where(ix == nx - 1, 0.5 * kx_last, 0.0)
-    share_coefs(line_x, (at_p, series, at_l), every_x)
-
     @pl.when(iy > 0)
     def _():
         edge_y_right().wait_recv()
@@ -347,6 +347,11 @@
     face_1 = 0.5 * (jnp.where(last, edge_y_in[1, 0], 0.0) + k1)
     flux_0 = face_0 * (jnp.where(inner, edge_y_in[0, 1], 0.0) - u0)
     flux_1 = face_1 * (jnp.where(last, edge_y_in[1, 1], 0.0) - u1)
+    at_p, series, at_l = factor_tree(*factor_cells(lambda t: gy[:, t], coef_y), tree_y)
+    at_l = at_l + jnp.where(iy == ny - 1, 0.5 * ky_last, 0.0)
+    share_coefs(line_y, (at_p, series, at_l), every_y)
+
+
     ends = jnp.concatenate([flux_0, flux_1], axis=0).T
     row = lax.broadcasted_iota(jnp.int32, (2 * groups, ly), 0)
     lane = lax.broadcasted_iota(jnp.int32, (2 * groups, ly), 1)
@@ -371,10 +376,9 @@
     send_values(line_x, d_p, d_l, out_x, got_x, mine_x)
 
     inverses = line_weights(ix, nx, chain_x, mine_x, weights_x)
-    at_p, series, at_l = factor_tree(*factor_cells(lambda t: gy[:, t], coef_y), tree_y)
-    at_l = at_l + jnp.where(iy == ny - 1, 0.5 * ky_last, 0.0)
-    share_coefs(line_y, (at_p, series, at_l), every_y)
-
+    await_coefs(line_y, every_y)
+    line_ratios(iy, ny, every_y, chain_y, mine_y)
+    inverses_y = line_weights(iy, ny, chain_y, mine_y, weights_y)
     u_p, u_l = take_values(line_x, inverses, out_x, got_x, weights_x)
     before, nodes = up_tree(u_p, u_l, tree_x, tkept_x)
 
@@ -391,11 +395,24 @@
 
     d_p, d_l = down_cells(y_cells, coef_y, kept_y)
     d_p, d_l = down_tree(d_p, d_l, tree_y, tkept_y)
-    await_coefs(line_y, every_y)
-    line_ratios(iy, ny, every_y, chain_y, mine_y)
     send_values(line_y, d_p, d_l, out_y, got_y, mine_y)
-    inverses = line_weights(iy, ny, chain_y, mine_y, weights_y)
-    u_p, u_l = take_values(line_y, inverses, out_y, got_y, weights_y)
+    line_x.done_sending(lambda o: every_x.at[ix], every_x, 0)
+    line_x.done_sending(lambda o: out_x.at[0], got_x, nx - 1)
+    line_y.done_sending(lambda o: every_y.at[iy], every_y, 0)
+
+    @pl.when(ix < nx - 1)
+    def _():
+        edge_x().wait_send()
+
+    @pl.when(iy < ny - 1)
+    def _():
+        edge_y_right().wait_send()
+
+    @pl.when(iy > 0)
+    def _():
+        edge_y_left().wait_send()
+
+    u_p, u_l = take_values(line_y, inverses_y, out_y, got_y, weights_y)
     before, nodes = up_tree(u_p, u_l, tree_y, tkept_y)
 
     def put_y(t, v):
@@ -406,21 +423,7 @@
     for g in range(groups):
         out_ref[g * lanes : (g + 1) * lanes] = group(u_raw, g) + 2.0 * turned[g * ly : (g + 1) * ly].T
 
-    for line, every, out, got in ((line_x, every_x, out_x, got_x), (line_y, every_y, out_y, got_y)):
-        line.done_sending(lambda o: every.at[line.me], every, 0)
-        line.done_sending(lambda o: out.at[0], got, line.n - 1)
-
-    @pl.when(ix < nx - 1)
-    def _():
-        edge_x().wait_send()
-
-    @pl.when(iy < ny - 1)
-    def _():
-        edge_y_right().wait_send()
-
-    @pl.when(iy > 0)
-    def _():
-        edge_y_left().wait_send()
+    line_y.done_sending(lambda o: out_y.at[0], got_y, ny - 1)
 
 
 def on_device(nx, ny, state, kappa_x, kappa_y):

time: 22 us -> 20.4 us (0.927)
  Pallas kernels: 21 us -> 19.5 us
    pallas_call x1, Pallas kernels: 21 us -> 19.5 us  [on_device(): pl.pallas_call(functools.partial(kernel, nx, ny, (nz, lx, ly)), out_shape...]
where the time goes in v9:
time: 20.4 us; the launch traced here: 20.3 us
  Pallas kernels  19.5 us (96%)
  local copies, waits for them, and re-layouts  0.8 us (4%)
    pallas_call x1, Pallas kernels, on_device(): pl.pallas_call(functools.partial(kernel, nx, ny, (nz, lx, ly)), out_shape...  19.5 us
    unnamed x1, local copies, waits for them, and re-layouts  0.8 us

profile of v9, /device:TPU:0, one launch (start us, length us, event | category | flops | bytes accessed | tf_op | source)
XLA Modules:
  0.0 20.3 jit_solution(14421419596958184470)
XLA Ops:
  0.0 19.5 %shard_map.37 = f32[1024,128]{1,0:T(8,128)S(1)} custom-call(f32[1024,128]{1,0:T(8,128)} %bitcast.5, f32[1024,128]{1,0:T(8,128)} %bitcast.6, f32[1024,128]{1,0:T(8,128)} %bitcast.7), custom_call_target="tpu_custom_call" | custom-call | tf_op jit(solution)/shard_map/pallas_call | solution.py:470
  19.5 0.8 %copy.5 = f32[16,64,128]{2,1,0:T(8,128)} copy(f32[16,64,128]{2,1,0:T(8,128)S(1)} %bitcast.4) | data formatting | bytes 1048576

commit v10 on v9

--- a/solution.py
+++ b/solution.py
@@ -15,6 +15,12 @@
 def recip(p):
     r = pl.reciprocal(p, approx=True)
     return r * (2.0 - p * r)
+
+
+def two_parts(v, axis):
+    high = v.astype(jnp.bfloat16)
+    low = (v - high.astype(F32)).astype(jnp.bfloat16)
+    return jnp.concatenate([high, low], axis=axis)
 
 
 def factor_cells(face, coef):
@@ -246,17 +252,17 @@
     bx, by = lx // SUB, ly // SUB
     ix = lax.axis_index("gx")
     iy = lax.axis_index("gy")
-    loads = []
-    for i, (src, dst) in enumerate(((ky_hbm, ky_raw), (u_hbm, u_raw), (kx_hbm, kx_raw))):
-        cp = pltpu.make_async_copy(src, dst, local_sem.at[i])
-        cp.start()
-        loads.append(cp)
     line_x = Line("gx", nx, ix, xs, xr)
     line_y = Line("gy", ny, iy, ys, yr)
     barrier = pltpu.get_barrier_semaphore()
     for line in (line_x, line_y):
         for _, target, _ in line.others():
             pl.semaphore_signal(barrier, inc=1, device_id={line.axis: target}, device_id_type=MESH)
+    loads = []
+    for i, (src, dst) in enumerate(((ky_hbm, ky_raw), (u_hbm, u_raw), (kx_hbm, kx_raw))):
+        cp = pltpu.make_async_copy(src, dst, local_sem.at[i])
+        cp.start()
+        loads.append(cp)
 
     def group(ref, g):
         return ref[g * lanes : (g + 1) * lanes]
@@ -279,15 +285,15 @@
     def edge_y_left():
         return line_y.copy(edge_y_out.at[0], edge_y_in.at[1], hy + 1, jnp.maximum(iy - 1, 0))
 
-    row8 = lax.broadcasted_iota(jnp.int32, (8, ly), 0)
-    lane8 = lax.broadcasted_iota(jnp.int32, (8, ly), 1)
-    pick = jnp.where(((row8 == 0) & (lane8 == 0)) | ((row8 == 1) & (lane8 == ly - 1)), 1.0, 0.0).astype(F32)
+    row16 = lax.broadcasted_iota(jnp.int32, (16, ly), 0)
+    lane16 = lax.broadcasted_iota(jnp.int32, (16, ly), 1)
+    pick = jnp.where(((row16 == 0) & (lane16 == 0)) | ((row16 == 1) & (lane16 == ly - 1)), 1.0, 0.0)
+    pick = jnp.concatenate([pick, pick], axis=1).astype(jnp.bfloat16)
     for kind, (load, raw) in enumerate(((loads[0], ky_raw), (loads[1], u_raw))):
         load.wait()
         for g in range(groups):
             edges = lax.dot_general(
-                pick, group(raw, g), (((1,), (1,)), ((), ())),
-                precision=lax.Precision.HIGHEST, preferred_element_type=F32,
+                pick, two_parts(group(raw, g), 1), (((1,), (1,)), ((), ())), preferred_element_type=F32
             )
             edge_y_out[0, kind, g : g + 1] = edges[0:1]
             edge_y_out[1, kind, g : g + 1] = edges[1:2]
@@ -352,15 +358,14 @@
     share_coefs(line_y, (at_p, series, at_l), every_y)
 
 
-    ends = jnp.concatenate([flux_0, flux_1], axis=0).T
+    ends = two_parts(jnp.concatenate([flux_0, flux_1], axis=0).T, 1)
     row = lax.broadcasted_iota(jnp.int32, (2 * groups, ly), 0)
     lane = lax.broadcasted_iota(jnp.int32, (2 * groups, ly), 1)
     inside = lax.broadcasted_iota(jnp.int32, (lanes, ly), 1) > 0
     for g in range(groups):
-        put = jnp.where(((row == g) & (lane == 0)) | ((row == groups + g) & (lane == ly - 1)), 1.0, 0.0).astype(F32)
-        added = lax.dot_general(
-            ends, put, (((1,), (0,)), ((), ())), precision=lax.Precision.HIGHEST, preferred_element_type=F32
-        )
+        put = jnp.where(((row == g) & (lane == 0)) | ((row == groups + g) & (lane == ly - 1)), 1.0, 0.0)
+        put = jnp.concatenate([put, put], axis=0).astype(jnp.bfloat16)
+        added = lax.dot_general(ends, put, (((1,), (0,)), ((), ())), preferred_element_type=F32)
         u = group(u_raw, g)
         k = group(ky_raw, g)
         flux = jnp.where(inside, 0.5 * (k + pltpu.roll(k, 1, 1)) * (u - pltpu.roll(u, 1, 1)), 0.0)

time: 20.4 us -> 20.4 us (level)
  no operation moved by 1% of the time
where the time goes in v10:
time: 20.4 us; the launch traced here: 20.3 us
  Pallas kernels  19.5 us (96%)
  local copies, waits for them, and re-layouts  0.8 us (4%)
    pallas_call x1, Pallas kernels, on_device(): pl.pallas_call(functools.partial(kernel, nx, ny, (nz, lx, ly)), out_shape...  19.5 us
    unnamed x1, local copies, waits for them, and re-layouts  0.8 us

profile of v10, /device:TPU:0, one launch (start us, length us, event | category | flops | bytes accessed | tf_op | source)
XLA Modules:
  0.0 20.3 jit_solution(7170370463536721139)
XLA Ops:
  0.0 19.5 %shard_map.37 = f32[1024,128]{1,0:T(8,128)S(1)} custom-call(f32[1024,128]{1,0:T(8,128)} %bitcast.5, f32[1024,128]{1,0:T(8,128)} %bitcast.6, f32[1024,128]{1,0:T(8,128)} %bitcast.7), custom_call_target="tpu_custom_call" | custom-call | tf_op jit(solution)/shard_map/pallas_call | solution.py:475
  19.5 0.8 %copy.5 = f32[16,64,128]{2,1,0:T(8,128)} copy(f32[16,64,128]{2,1,0:T(8,128)S(1)} %bitcast.4) | data formatting | bytes 1048576

commit v11 on v10

--- a/solution.py
+++ b/solution.py
@@ -192,7 +192,7 @@
         )
 
     def others(self):
-        for o in range(1, self.n):
+        for o in sorted(range(1, self.n), key=lambda o: abs(2 * o - self.n)):
             yield o, lax.rem(self.me + o, self.n), lax.rem(self.me + self.n - o, self.n)
 
     def start_all(self, src_of, buf, base):
@@ -229,7 +229,7 @@
 def take_values(line, inverses, out, got, weights):
     u_p = inverses[0] * out[1]
     u_l = inverses[1] * out[0]
-    for o, _, source in line.others():
+    for o, _, source in reversed(list(line.others())):
         line.await_one(o, out.at[0], got, line.n - 1)
         v = got[source]
         u_p = u_p + weights[source, 0] * v
@@ -243,7 +243,7 @@
     u_raw, kx_raw, ky_raw, nat, turned, gx, gy,
     coef_x, kept_x, tree_x, tkept_x, every_x, weights_x, chain_x, mine_x, out_x, got_x,
     coef_y, kept_y, tree_y, tkept_y, every_y, weights_y, chain_y, mine_y, out_y, got_y,
-    edge_x_out, edge_x_in, edge_y_out, edge_y_in,
+    edge_x_in, edge_y_out, edge_y_in,
     local_sem, xs, xr, ys, yr,
 ):
     nz, lx, ly = dims
@@ -277,7 +277,7 @@
     hy = 2 * (ny - 1)
 
     def edge_x():
-        return line_x.copy(edge_x_out, edge_x_in, hx, jnp.minimum(ix + 1, nx - 1))
+        return line_x.copy(kx_hbm.reshape(nz, lx, ly).at[:, lx - 1, :], edge_x_in, hx, jnp.minimum(ix + 1, nx - 1))
 
     def edge_y_right():
         return line_y.copy(edge_y_out.at[1], edge_y_in.at[0], hy, jnp.minimum(iy + 1, ny - 1))
@@ -297,23 +297,23 @@
             )
             edge_y_out[0, kind, g : g + 1] = edges[0:1]
             edge_y_out[1, kind, g : g + 1] = edges[1:2]
+    pl.semaphore_wait(barrier, nx - 1 + ny - 1)
+
+    @pl.when(ix < nx - 1)
+    def _():
+        edge_x().start()
+
+    @pl.when(iy < ny - 1)
+    def _():
+        edge_y_right().start()
+
+    @pl.when(iy > 0)
+    def _():
+        edge_y_left().start()
+
     loads[2].wait()
     kx_first = x_rows(kx_raw, 0)
     kx_last = x_rows(kx_raw, lx - 1)
-    edge_x_out[...] = kx_last
-    pl.semaphore_wait(barrier, nx - 1 + ny - 1)
-
-    @pl.when(ix < nx - 1)
-    def _():
-        edge_x().start()
-
-    @pl.when(iy < ny - 1)
-    def _():
-        edge_y_right().start()
-
-    @pl.when(iy > 0)
-    def _():
-        edge_y_left().start()
 
     prior = kx_first
     for x in range(1, lx):
@@ -461,7 +461,6 @@
         + line_scratch(nx, bx, nz)
         + line_scratch(ny, by, groups)
         + [
-            pltpu.VMEM((nz, ly), F32),
             pltpu.VMEM((nz, ly), F32),
             pltpu.VMEM((2, 2, groups, 128), F32),
             pltpu.VMEM((2, 2, groups, 128), F32),

time: 20.4 us -> 20.6 us (level)
  no operation moved by 1% of the time
where the time goes in v11:
time: 20.6 us; the launch traced here: 20.4 us
  Pallas kernels  19.6 us (95%)
  local copies, waits for them, and re-layouts  0.8 us (4%)
    pallas_call x1, Pallas kernels, on_device(): pl.pallas_call(functools.partial(kernel, nx, ny, (nz, lx, ly)), out_shape...  19.6 us
    unnamed x1, local copies, waits for them, and re-layouts  0.8 us

profile of v11, /device:TPU:0, one launch (start us, length us, event | category | flops | bytes accessed | tf_op | source)
XLA Modules:
  0.0 20.4 jit_solution(8239815947761075922)
XLA Ops:
  0.0 19.6 %shard_map.37 = f32[1024,128]{1,0:T(8,128)S(1)} custom-call(f32[1024,128]{1,0:T(8,128)} %bitcast.5, f32[1024,128]{1,0:T(8,128)} %bitcast.6, f32[1024,128]{1,0:T(8,128)} %bitcast.7), custom_call_target="tpu_custom_call" | custom-call | tf_op jit(solution)/shard_map/pallas_call | solution.py:474
  19.7 0.8 %copy.5 = f32[16,64,128]{2,1,0:T(8,128)} copy(f32[16,64,128]{2,1,0:T(8,128)S(1)} %bitcast.4) | data formatting | bytes 1048576

commit v12 on v10

--- a/solution.py
+++ b/solution.py
@@ -297,23 +297,24 @@
             )
             edge_y_out[0, kind, g : g + 1] = edges[0:1]
             edge_y_out[1, kind, g : g + 1] = edges[1:2]
+    pl.semaphore_wait(barrier, nx - 1 + ny - 1)
+
+    @pl.when(iy < ny - 1)
+    def _():
+        edge_y_right().start()
+
+    @pl.when(iy > 0)
+    def _():
+        edge_y_left().start()
+
     loads[2].wait()
     kx_first = x_rows(kx_raw, 0)
     kx_last = x_rows(kx_raw, lx - 1)
     edge_x_out[...] = kx_last
-    pl.semaphore_wait(barrier, nx - 1 + ny - 1)
 
     @pl.when(ix < nx - 1)
     def _():
         edge_x().start()
-
-    @pl.when(iy < ny - 1)
-    def _():
-        edge_y_right().start()
-
-    @pl.when(iy > 0)
-    def _():
-        edge_y_left().start()
 
     prior = kx_first
     for x in range(1, lx):

time: 20.4 us -> 20.4 us (level)
  no operation moved by 1% of the time
where the time goes in v12:
time: 20.4 us; the launch traced here: 20.3 us
  Pallas kernels  19.5 us (96%)
  local copies, waits for them, and re-layouts  0.8 us (4%)
    pallas_call x1, Pallas kernels, on_device(): pl.pallas_call(functools.partial(kernel, nx, ny, (nz, lx, ly)), out_shape...  19.5 us
    unnamed x1, local copies, waits for them, and re-layouts  0.8 us

profile of v12, /device:TPU:0, one launch (start us, length us, event | category | flops | bytes accessed | tf_op | source)
XLA Modules:
  0.0 20.3 jit_solution(165632753167949575)
XLA Ops:
  0.0 19.5 %shard_map.37 = f32[1024,128]{1,0:T(8,128)S(1)} custom-call(f32[1024,128]{1,0:T(8,128)} %bitcast.5, f32[1024,128]{1,0:T(8,128)} %bitcast.6, f32[1024,128]{1,0:T(8,128)} %bitcast.7), custom_call_target="tpu_custom_call" | custom-call | tf_op jit(solution)/shard_map/pallas_call | solution.py:476
  19.5 0.8 %copy.5 = f32[16,64,128]{2,1,0:T(8,128)} copy(f32[16,64,128]{2,1,0:T(8,128)S(1)} %bitcast.4) | data formatting | bytes 1048576
